TPU v7x, 256 devices: a whole 4x4x8 slice. The times are simulated.
256 devices in a mesh: grp: 16 (over z, core), loc: 16 (over x, y).
Axes of the slice: x: 4, y: 4, z: 8, core: 2. Of those that a mesh axis runs over, the one named last changes fastest.
Arguments:
- right_side: float32 [256, 512, 256], P('grp', 'loc'), may hold values from -6 to 6
- phase: int32 [256, 512, 256], P('grp', 'loc'), may hold values 0 or 1
Outputs:
- fine_residual: float32 [256, 512, 256], P('grp', 'loc')
- coarse_residual: float32 [32, 64, 32], P('grp')
All inputs are finite; a program needn't handle non-finite values. No bound on the sum of `phase` on one device may be relied on, other than what follows from the above.
Results may differ from a plain program's by a relative error of at most 0.000027.
Values sent between devices are 32-bit elements; how exact they have to be, the bound alone decides.
A program may use at most 64 MiB of HBM per device.

v0:
```python
import functools

import jax
import jax.numpy as jnp
from jax import lax
from jax.experimental import pallas as pl
from jax.experimental.pallas import tpu as pltpu
from jax.sharding import PartitionSpec as P

MESH = pl.DeviceIdType.MESH
NG, NL = 16, 16
COARSE_SWEEPS = 4
F32 = jnp.float32
BF16 = jnp.bfloat16
WHOLE = ((256, 512, 256), (128, 256, 128), (64, 128, 64), (32, 64, 32))
BLOCK = ((16, 32, 256), (8, 16, 128), (4, 8, 64), (2, 64, 32))
LOW = (4, 4, 12, 5)
PLANES = (22, 14, 28, 11)
ROWS = (40, 24, 16, 72)
LANES = (256, 128, 128, 128)

NEAR = [(a, b) for a in (-1, 0, 1) for b in (-1, 0, 1) if (a, b) != (0, 0)]
WIDE = [(a, b) for a in range(-3, 4) for b in (-1, 0, 1) if (a, b) != (0, 0)]
ALONG = [(0, k) for k in range(1, NL)]
GREET = [(a, b % NL) for a, b in WIDE] + [(0, k) for k in range(2, NL - 1)]


def lane_ids(shape):
    return lax.broadcasted_iota(jnp.int32, shape, len(shape) - 1)


def row_ids(shape):
    return lax.broadcasted_iota(jnp.int32, shape, len(shape) - 2)


def split_dot(values, matrix):
    high = values.astype(BF16)
    rest = values - high.astype(F32)
    mid = rest.astype(BF16)
    low = (rest - mid.astype(F32)).astype(BF16)
    dot = functools.partial(jnp.dot, preferred_element_type=F32)
    return dot(high, matrix) + (dot(mid, matrix) + dot(low, matrix))


class Level:
    def __init__(self, index, g, l, refs):
        self.index = index
        self.F, self.C, self.U, self.V, self.Ei, self.Ej, self.El, self.K5, self.W = refs
        self.n = BLOCK[index]
        self.low = LOW[index]
        self.rows, self.lanes = ROWS[index], LANES[index]
        self.g, self.l = g, l

    def up(self, x, axis):
        return pltpu.roll(x, x.shape[axis] - 1, axis)

    def down(self, x, axis):
        return pltpu.roll(x, 1, axis)

    def lane_up(self, x):
        y = self.up(x, x.ndim - 1)
        return jnp.where(lane_ids(y.shape) == self.n[2] - 1, 0.0, y) if self.n[2] == self.lanes else y

    def lane_down(self, x):
        y = self.down(x, x.ndim - 1)
        return jnp.where(lane_ids(y.shape) == 0, 0.0, y) if self.n[2] == self.lanes else y

    def row_up(self, x):
        return self.up(x, x.ndim - 2)

    def row_down(self, x):
        return self.down(x, x.ndim - 2)

    def row_valid(self, shape):
        r = row_ids(shape)
        if self.index == 3:
            ok = r < self.n[1]
        else:
            j = jnp.where(r < self.n[1] + 4, r, r - self.rows) + self.l * self.n[1]
            ok = (j >= 0) & (j < WHOLE[self.index][1])
        if self.n[2] < self.lanes:
            ok = ok & (lane_ids(shape) < self.n[2])
        return jnp.where(ok, 1.0, 0.0).astype(F32)

    def plane_valid(self, i):
        p = self.g * self.n[0] + (i - self.low)
        return jnp.where((p >= 0) & (p < WHOLE[self.index][0]), 1.0, 0.0).astype(F32)

    def plane_valid_many(self, lo, hi):
        shape = (hi - lo, self.rows, self.lanes)
        p = self.g * self.n[0] + (lo - self.low) + lax.broadcasted_iota(jnp.int32, shape, 0)
        return jnp.where((p >= 0) & (p < WHOLE[self.index][0]), 1.0, 0.0).astype(F32)

    def cells(self, c):
        cl = c + self.lane_down(c)
        cj = c + self.row_down(c)
        cjl = cl + self.row_down(cl)
        return cl, cj, cjl

    def coefficients(self, cells, before, valid):
        cl, cj, cjl = cells
        pl_, pj, pjl = before
        k = cjl + pjl
        el = cj + pj
        if self.n[2] == self.lanes:
            el = jnp.where(lane_ids(el.shape) == self.n[2] - 1, 0.0, el)
        return cjl, cl + pl_, el, 5.0 * k, valid * (0.15 / jnp.maximum(k, 1.0))

    def parts(self, u):
        ul = self.lane_up(u)
        uj = self.row_up(u)
        a = u + ul
        return ul, uj, a + self.row_up(a)

    def combine(self, u, un, up, ul, uj, t, ei, eip, ej, el, k5):
        tj = t + self.row_down(t)
        b = k5 * u + ei * un + eip * up + ej * uj + el * ul - tj
        return b + self.lane_down(el * u - tj) + self.row_down(ej * u)

    def setup_all(self, lo, hi):
        cl, cj, cjl = self.cells(self.C[lo - 1:hi])
        valid = self.row_valid((1, self.rows, self.lanes)) * self.plane_valid_many(lo, hi)
        ei, ej, el, k5, w = self.coefficients(
            (cl[1:], cj[1:], cjl[1:]), (cl[:-1], cj[:-1], cjl[:-1]), valid
        )
        self.Ei[lo - 1:hi] = cjl
        self.Ej[lo:hi] = ej
        self.El[lo:hi] = el
        self.K5[lo:hi] = k5
        self.W[lo:hi] = w

    def apply_all(self, u_ref, lo, hi):
        u = u_ref[lo - 1:hi + 1]
        ul, uj, v = self.parts(u)
        t = self.C[lo - 1:hi] * (v[:-1] + v[1:])
        return self.combine(
            u[1:-1], u[2:], u[:-2], ul[1:-1], uj[1:-1], t[1:] + t[:-1],
            self.Ei[lo:hi], self.Ei[lo - 1:hi - 1], self.Ej[lo:hi], self.El[lo:hi], self.K5[lo:hi],
        )

    def first_all(self, lo, hi):
        self.U[lo:hi] = self.W[lo:hi] * self.F[lo:hi]

    def sweep_all(self, source, target, lo, hi):
        b = self.apply_all(source, lo, hi)
        target[lo:hi] = source[lo:hi] + self.W[lo:hi] * (self.F[lo:hi] - b)

    def residual_all(self, source, lo, hi):
        return self.F[lo:hi] - self.apply_all(source, lo, hi)

    def planes_loop(self, lo, hi, step, carry, unroll):
        whole = (hi - lo) // unroll

        def body(k, c):
            for m in range(unroll):
                c = step(lo + k * unroll + m, c)
            return c

        carry = lax.fori_loop(0, whole, body, carry)
        for i in range(lo + whole * unroll, hi):
            carry = step(i, carry)
        return carry

    def apply_loop(self, u_ref, lo, hi, emit, unroll):
        _, _, v0 = self.parts(u_ref[lo - 1])
        ul, uj, v = self.parts(u_ref[lo])
        t = self.C[lo - 1] * (v0 + v)

        def step(i, carry):
            ul, uj, v, t = carry
            u = u_ref[i]
            un = u_ref[i + 1]
            uln, ujn, vn = self.parts(un)
            tn = self.C[i] * (v + vn)
            b = self.combine(
                u, un, u_ref[i - 1], ul, uj, t + tn,
                self.Ei[i], self.Ei[i - 1], self.Ej[i], self.El[i], self.K5[i],
            )
            emit(i, u, b)
            return uln, ujn, vn, tn

        self.planes_loop(lo, hi, step, (ul, uj, v, t), unroll)


def kernel(*refs):
    (rhs, phase, r0_mat, r1_mat, r2_mat, p0_mat, p1_mat, fine_out, coarse_out) = refs[:9]
    refs = refs[9:]
    windows = [refs[9 * k:9 * k + 9] for k in range(4)]
    (
        ph, upk, dpk, rxl0, rxh0, rs, s0, out, ct1, n1, h0,
        rxl1, rxh1, crl1, crh1, c1w, s1, ct2, pf2, pn2, rf2, rn2, n2w, n3s, s2, pf3, pc3, rf3, rc3,
        lsem, ss0, rs0, sf1, qf1, sc1, qc1, sf2, qf2, sc2, qc2, sf3, qf3, sc3, qc3,
    ) = refs[36:]
    g = lax.axis_index("grp")
    l = lax.axis_index("loc")
    lv = [Level(k, g, l, windows[k]) for k in range(4)]
    L0, L1, L2, L3 = lv
    sent = []

    def device(dg, dl):
        return lax.rem(g + dg + NG, NG), lax.rem(l + dl + NL, NL)

    def send(src, dst, s_sem, r_sem, to):
        copy = pltpu.make_async_remote_copy(
            src_ref=src, dst_ref=dst, send_sem=s_sem, recv_sem=r_sem,
            device_id=device(*to), device_id_type=MESH,
        )
        copy.start()
        sent.append(copy)
        return copy

    load_f = pltpu.make_async_copy(rhs, L0.F.at[4:20, 0:32], lsem.at[0])
    load_p = pltpu.make_async_copy(phase, ph, lsem.at[1])
    load_p.start()
    load_f.start()
    barrier = pltpu.get_barrier_semaphore()
    for to in GREET:
        pl.semaphore_signal(barrier, inc=1, device_id=device(*to), device_id_type=MESH)

    load_p.wait()
    gas = ph[...].astype(F32)
    L0.C[4:20, 0:32] = 1.0 + 999.0 * gas
    pairs = jnp.concatenate([gas[2 * i:2 * i + 1] + gas[2 * i + 1:2 * i + 2] for i in range(8)], 0)
    ct1[...] = jnp.dot(
        pairs.reshape(8 * 32, 256).astype(BF16), p0_mat[...], preferred_element_type=F32
    ).reshape(8, 32, 128)
    n1[...] = ct1[:, pl.ds(0, 16, stride=2), :] + ct1[:, pl.ds(1, 16, stride=2), :]
    count1 = n1[...]
    L1.C[4:12, 0:16] = 1.0 + 124.875 * count1
    pairs = jnp.concatenate([count1[2 * i:2 * i + 1] + count1[2 * i + 1:2 * i + 2] for i in range(4)], 0)
    ct2[...] = jnp.dot(
        pairs.reshape(4 * 16, 128).astype(BF16), p1_mat[...], preferred_element_type=F32
    ).reshape(4, 16, 128)
    count2 = ct2[:, pl.ds(0, 8, stride=2), :] + ct2[:, pl.ds(1, 8, stride=2), :]
    pn2[...] = count2[0:2] + pltpu.roll(count2[2:4], 64, 2)
    rn2[3, 1] = pn2[...]

    load_f.wait()
    sub = row_ids((1, 8, 256)) < 4
    upk[...] = jnp.where(sub, pltpu.roll(L0.C[4:20, 24:32], 4, 1), L0.F[4:20, 24:32])
    dpk[...] = jnp.where(sub, L0.F[4:20, 0:8], pltpu.roll(L0.C[4:20, 0:8], 4, 1))
    for ref in (L3.F, L3.C):
        ref[:, 64:72] = jnp.zeros((PLANES[3], 8, 128), F32)

    pl.semaphore_wait(barrier, len(GREET))

    first = []
    k = 0
    for src, dst, to in (
        (upk, rxl0.at[4:20], (0, 1)),
        (dpk, rxh0.at[4:20], (0, -1)),
        (L0.C.at[16:20, 0:32], L0.C.at[0:4, 0:32], (1, 0)),
        (L0.F.at[17:20, 0:32], L0.F.at[1:4, 0:32], (1, 0)),
        (L0.C.at[4:6, 0:32], L0.C.at[20:22, 0:32], (-1, 0)),
        (L0.F.at[4:6, 0:32], L0.F.at[20:22, 0:32], (-1, 0)),
        (upk.at[12:16], rxl0.at[0:4], (1, 1)),
        (dpk.at[12:16], rxh0.at[0:4], (1, -1)),
        (upk.at[0:2], rxl0.at[20:22], (-1, 1)),
        (dpk.at[0:2], rxh0.at[20:22], (-1, -1)),
    ):
        first.append(send(src, dst, ss0.at[k], rs0.at[k], to))
        k += 1

    def near_sends(ref, low, high, ssem, rsem, depth):
        copies = []
        for k, (dg, dl) in enumerate(NEAR):
            lo, hi, at = {1: (12 - depth, 12, 4 - depth), 0: (4, 12, 4), -1: (4, 6, 12)}[dg]
            rows, target = {1: (slice(8, 16), low), 0: (slice(0, 16), ref), -1: (slice(0, 8), high)}[dl]
            where = pl.ds(at, hi - lo)
            dst = target.at[where, 0:16] if dl == 0 else target.at[where]
            copies.append(send(ref.at[lo:hi, rows], dst, ssem.at[k], rsem.at[k], (dg, dl)))
        return copies

    def wide_sends(src, slots, ssem, rsem):
        return [
            send(src, slots.at[3 - dg, 1 - dl], ssem.at[k], rsem.at[k], (dg, dl))
            for k, (dg, dl) in enumerate(WIDE)
        ]

    def along_sends(src, slots, ssem, rsem):
        mine = slots.at[lax.div(l, 2), lax.rem(l, 2)]
        return [send(src, mine, ssem.at[k], rsem.at[k], to) for k, to in enumerate(ALONG)]

    got_c1 = near_sends(L1.C, crl1, crh1, sc1, qc1, 4)
    got_c2 = wide_sends(pn2, rn2, sc2, qc2)

    for copy in first:
        copy.wait_recv()
    rows0 = L0.row_valid((40, 256))
    sub = row_ids((8, 256)) < 4

    def merge(i, _):
        low, high = rxl0[i], rxh0[i]
        L0.F[i, 32:40] = jnp.where(sub, high, low)
        L0.C[i, 32:40] = pltpu.roll(jnp.where(sub, low, high), 4, 0) * rows0[32:40] * L0.plane_valid(i)
        return 0

    lax.fori_loop(0, 22, merge, 0)
    for i in (0, 1, 2, 3, 20, 21):
        L0.C[i, 0:32] = L0.C[i, 0:32] * L0.plane_valid(i)

    def setup(i, before):
        cells = L0.cells(L0.C[i])
        ei, ej, el, k5, w = L0.coefficients(cells, before, rows0 * L0.plane_valid(i))
        L0.Ei[i], L0.Ej[i], L0.El[i], L0.K5[i], L0.W[i] = ei, ej, el, k5, w
        L0.U[i] = w * (12.0 * L0.F[i])
        return cells

    before = L0.cells(L0.C[0])
    L0.Ei[0] = before[2]
    L0.planes_loop(1, 22, setup, before, 3)

    def second(i, u, b):
        L0.V[i] = u + L0.W[i] * (12.0 * L0.F[i] - b)

    L0.apply_loop(L0.U, 2, 21, second, 3)

    def residual(i, u, b):
        r = (12.0 * L0.F[i] - b) * (rows0 * L0.plane_valid(i))
        rs[i - 3, 0:8] = r[32:40]
        rs[i - 3, 8:40] = r[0:32]
        out[jnp.maximum(i - 4, 0)] = r[0:32] * (1.0 / 12.0)

    L0.apply_loop(L0.V, 3, 20, residual, 3)
    store = pltpu.make_async_copy(out, fine_out, lsem.at[2])
    store.start()

    def restrict(scratch, matrix, planes, rows, lanes, kept):
        scratch_r, scratch_s = scratch
        scratch_s[...] = split_dot(scratch_r.reshape(planes * rows, lanes), matrix).reshape(planes, rows, 128)
        h = 0.5 * (
            scratch_s[:, pl.ds(7, kept, stride=2), :] + scratch_s[:, pl.ds(9, kept, stride=2), :]
        ) + scratch_s[:, pl.ds(8, kept, stride=2), :]
        count = (planes - 1) // 2
        return [0.5 * (h[2 * i] + h[2 * i + 2]) + h[2 * i + 1] for i in range(count)]

    f1 = restrict((rs[...], s0), r0_mat[...], 17, 40, 256, 16)
    for i in range(8):
        L1.F[4 + i, 0:16] = f1[i]
    got_f1 = near_sends(L1.F, rxl1, rxh1, sf1, qf1, 3)

    for copy in got_c1:
        copy.wait_recv()
    sub1 = row_ids((1, 8, 128)) < 4
    valid1 = L1.row_valid((1, 24, 128)) * L1.plane_valid_many(0, 14)
    c1w[:, 0:16] = L1.C[:, 0:16] * valid1[:, 0:16]
    c1w[:, 16:24] = jnp.where(sub1, crh1[...], crl1[...]) * valid1[:, 16:24]
    L1.C = c1w
    L1.setup_all(1, 14)

    def unpack_wide(slots, put):
        lane = lane_ids((1, 1, 1, 128)) < 64
        own = slots[:, 1]
        halo = jnp.where(row_ids((1, 1, 8, 128)) < 4, slots[:, 2], slots[:, 0])
        for tile, rows in ((own, slice(0, 8)), (halo, slice(8, 16))):
            first = jnp.where(lane, tile, 0.0)
            later = jnp.where(lane, pltpu.roll(tile, 64, 3), 0.0)
            for d in range(7):
                for half in range(2):
                    put(4 * d + half, rows, first[d, half])
                    put(4 * d + 2 + half, rows, later[d, half])

    for copy in got_c2:
        copy.wait_recv()

    def put_n2(i, rows, value):
        n2w[i, rows] = value

    unpack_wide(rn2, put_n2)
    valid2 = L2.row_valid((1, 16, 128)) * L2.plane_valid_many(0, 28)
    L2.C[...] = (1.0 + (999.0 / 64.0) * n2w[...]) * valid2
    L2.setup_all(1, 26)

    count2 = n2w[2:24, 0:8]
    pairs = jnp.concatenate([count2[2 * i:2 * i + 1] + count2[2 * i + 1:2 * i + 2] for i in range(11)], 0)
    n3s[...] = jnp.dot(
        pairs.reshape(11 * 8, 128).astype(BF16), p1_mat[...], preferred_element_type=F32
    ).reshape(11, 8, 128)
    count3 = n3s[:, pl.ds(0, 4, stride=2), :] + n3s[:, pl.ds(1, 4, stride=2), :]

    odd = lax.rem(l, 2) == 1

    def pack(planes, ref):
        for t in range(2):
            for h in range(2):
                total = jnp.zeros((4, 128), F32)
                for q in range(4):
                    p = 8 * t + 4 * h + q
                    if p < len(planes):
                        total = total + (pltpu.roll(planes[p], 32 * q, 1) if q else planes[p])
                ref[t, 4 * h:4 * h + 4] = total
        tiles = ref[...]
        ref[...] = jnp.where(odd, pltpu.roll(tiles, 4, 1), tiles)

    def unpack_along(slots, count, put):
        sub = row_ids((1, 8, 128)) < 4
        lane = lane_ids((1, 8, 128)) < 32
        for p in range(count):
            t, h, q = p // 8, (p % 8) // 4, p % 4
            even, other = slots[:, 0, t], slots[:, 1, t]
            tile = jnp.where(sub, even, other) if h == 0 else pltpu.roll(jnp.where(sub, other, even), 4, 1)
            if q:
                tile = pltpu.roll(tile, 128 - 32 * q, 2)
            put(p, jnp.where(lane, tile, 0.0).reshape(64, 128))

    pack([count3[i] for i in range(11)], pc3)
    rc3[lax.div(l, 2), lax.rem(l, 2)] = pc3[...]
    got_c3 = along_sends(pc3, rc3, sc3, qc3)

    for copy in got_f1:
        copy.wait_recv()
    L1.F[1:14, 16:24] = jnp.where(sub1, rxh1[1:14], rxl1[1:14])
    L1.first_all(1, 14)
    L1.sweep_all(L1.U, L1.V, 2, 13)
    r1 = L1.residual_all(L1.V, 3, 12) * valid1[3:12]
    r1 = jnp.concatenate([r1[:, 16:24], r1[:, 0:16]], 1)
    f2 = restrict((r1, s1), r1_mat[...], 9, 24, 128, 8)
    pf2[...] = jnp.concatenate([x[None] for x in f2[0:2]], 0) + pltpu.roll(
        jnp.concatenate([x[None] for x in f2[2:4]], 0), 64, 2
    )
    rf2[3, 1] = pf2[...]
    got_f2 = wide_sends(pf2, rf2, sf2, qf2)

    for copy in got_c3:
        copy.wait_recv()

    def put_c3(p, value):
        L3.C[p, 0:64] = (1.0 + (999.0 / 512.0) * value) * (
            L3.row_valid((72, 128))[0:64] * L3.plane_valid(p)
        )

    unpack_along(rc3, 11, put_c3)
    L3.setup_all(1, 11)

    for copy in got_f2:
        copy.wait_recv()

    def put_f2(i, rows, value):
        L2.F[i, rows] = value

    unpack_wide(rf2, put_f2)
    L2.first_all(1, 26)
    L2.sweep_all(L2.U, L2.V, 2, 25)
    r2 = L2.residual_all(L2.V, 3, 24) * valid2[3:24]
    r2 = jnp.concatenate([r2[:, 8:16], r2[:, 0:8]], 1)
    f3 = restrict((r2, s2), r2_mat[...], 21, 16, 128, 4)
    pack(f3, pf3)
    rf3[lax.div(l, 2), lax.rem(l, 2)] = pf3[...]
    got_f3 = along_sends(pf3, rf3, sf3, qf3)
    for copy in got_f3:
        copy.wait_recv()

    def put_f3(p, value):
        L3.F[p + 1, 0:64] = value

    unpack_along(rf3, 10, put_f3)
    L3.first_all(1, 11)
    source, target = L3.U, L3.V
    for sweep in range(COARSE_SWEEPS - 1):
        L3.sweep_all(source, target, 2 + sweep, 10 - sweep)
        source, target = target, source
    coarse_out[...] = ((8.0 / 12.0) * L3.residual_all(source, 5, 7))[:, 0:64, 0:32]

    store.wait()
    for copy in sent:
        copy.wait_send()


def lane_matrices():
    def weights(size, used):
        k = jnp.arange(size)[:, None]
        c = jnp.arange(128)[None, :]
        live = (k < used) & (c < used // 2)
        near = jnp.abs(k - 2 * c)
        full = jnp.where(live, jnp.where(near == 0, 0.5, jnp.where(near == 1, 0.25, 0.0)), 0.0)
        return full.astype(BF16)

    def sums(size):
        k = jnp.arange(size)[:, None]
        c = jnp.arange(128)[None, :]
        return jnp.where(k // 2 == c, 1.0, 0.0).astype(BF16)

    return weights(256, 256), weights(128, 128), weights(128, 64), sums(256), sums(128)


def per_device(right_side, phase):
    scratch = []
    for k in range(4):
        shape = (PLANES[k], ROWS[k], LANES[k])
        scratch += [pltpu.VMEM(shape, F32) for _ in range(9)]
    scratch += [
        pltpu.VMEM(s, d)
        for s, d in (
            ((16, 32, 256), jnp.int32),
            ((16, 8, 256), F32), ((16, 8, 256), F32),
            ((22, 8, 256), F32), ((22, 8, 256), F32),
            ((17, 40, 256), F32), ((17, 40, 128), F32),
            ((16, 32, 256), F32),
            ((8, 32, 128), F32), ((8, 16, 128), F32), ((17, 16, 128), F32),
            ((14, 8, 128), F32), ((14, 8, 128), F32), ((14, 8, 128), F32), ((14, 8, 128), F32),
            ((14, 24, 128), F32),
            ((9, 24, 128), F32),
            ((4, 16, 128), F32),
            ((2, 8, 128), F32), ((2, 8, 128), F32),
            ((7, 3, 2, 8, 128), F32), ((7, 3, 2, 8, 128), F32),
            ((28, 16, 128), F32), ((11, 8, 128), F32), ((21, 16, 128), F32),
            ((2, 8, 128), F32), ((2, 8, 128), F32),
            ((8, 2, 2, 8, 128), F32), ((8, 2, 2, 8, 128), F32),
        )
    ]
    scratch.append(pltpu.SemaphoreType.DMA((3,)))
    for n in (10, len(NEAR), len(NEAR), len(WIDE), len(WIDE), len(ALONG), len(ALONG)):
        scratch += [pltpu.SemaphoreType.DMA((n,)), pltpu.SemaphoreType.DMA((n,))]
    vmem = pl.BlockSpec(memory_space=pltpu.VMEM)
    hbm = pl.BlockSpec(memory_space=pl.ANY)
    return pl.pallas_call(
        kernel,
        out_shape=(
            jax.ShapeDtypeStruct((16, 32, 256), F32),
            jax.ShapeDtypeStruct((2, 64, 32), F32),
        ),
        in_specs=[hbm, hbm] + [vmem] * 5,
        out_specs=(hbm, vmem),
        scratch_shapes=scratch,
        compiler_params=pltpu.CompilerParams(
            collective_id=0, has_side_effects=True, vmem_limit_bytes=56 * 2**20
        ),
    )(right_side, phase, *lane_matrices())


def solution(mesh):
    in_specs = (P("grp", "loc", None), P("grp", "loc", None))
    out_specs = (P("grp", "loc", None), P("grp", None, None))
    return jax.shard_map(
        per_device, mesh=mesh, in_specs=in_specs, out_specs=out_specs, check_vma=False
    )
```

profile of v0, /device:TPU:1, one launch (start us, length us, event | category | flops | bytes accessed | tf_op | source)
XLA Modules:
  0.0 51.4 jit_solution(14103566662883496982)
XLA Ops:
  0.7 0.7 %select_convert_fusion.2.refs_6_ = bf16[128,128]{1,0:T(8,128)(2,1)} fusion(s32[128]{0:T(128)S(1)} %and_select_fusion), kind=kLoop, calls=%fused_computation.6 | loop fusion | flops 49152 | bytes 33280 | tf_op jit(solution)/shard_map/convert_element_type | solution.py:481
  1.4 0.7 %select_convert_fusion.3 = (bf16[128,128]{1,0:T(8,128)(2,1)}, bf16[128,128]{1,0:T(8,128)(2,1)}) fusion(s32[128]{0:T(128)S(1)} %iota_multiply_fusion, pred[128]{0:T(512)(128)(4,1)S(1)} %get-tuple-element.6, pred[128]{0:T(512)(128)(4,1)S(1)} %get-tuple-element.7, pred[128]{0:T(512)(128)(4,1)S(1)} %iota_compare_fusion.5), kind=kLoop, calls=%fused_computation.8 | loop fusion | flops 196608 | bytes 66432 | tf_op jit(solution)/shard_map/convert_element_type | solution.py:476
  2.1 0.8 %select_convert_fusion = (bf16[256,128]{1,0:T(8,128)(2,1)}, bf16[256,128]{1,0:T(8,128)(2,1)}) fusion(s32[256]{0:T(256)S(1)} %and_select_fusion.1, s32[128]{0:T(128)S(1)} %iota_multiply_fusion, pred[128]{0:T(512)(128)(4,1)S(1)} %iota_compare_fusion.5, pred[256]{0:T(512)(128)(4,1)S(1)} %iota_compare_fusion.2), kind=kLoop, calls=%fused_computation | loop fusion | flops 393216 | bytes 132992 | tf_op jit(solution)/shard_map/convert_element_type | solution.py:481
  2.9 45.2 %shard_map.41 = (f32[16,32,256]{2,1,0:T(8,128)}, f32[2,64,32]{2,1,0:T(8,128)}) custom-call(f32[16,32,256]{2,1,0:T(8,128)} %refs_0_.1, s32[16,32,256]{2,1,0:T(8,128)} %refs_1_.1, bf16[256,128]{1,0:T(8,128)(2,1)} %get-tuple-element.9.refs_2_, bf16[128,128]{1,0:T(8,128)(2,1)} %get-tuple-element.5.refs_3_, bf16[128,128]{1,0:T(8,128)(2,1)} %get-tuple-element.4.refs_4_, ...), custom_call_target="tpu_custom_call" | custom-call | tf_op jit(solution)/shard_map/pallas_call | solution.py:516
  48.0 1.5 %copy.4 = f32[2,64,32]{1,2,0:T(8,128)} copy(f32[2,64,32]{2,1,0:T(8,128)} %get-tuple-element.3) | data formatting | bytes 32768 | tf_op jit(solution)/shard_map/pallas_call | solution.py:516
  49.6 1.9 %copy.6 = f32[16,32,256]{2,1,0:T(8,128)} copy(f32[16,32,256]{2,1,0:T(8,128)} %get-tuple-element.12) | data formatting | bytes 1048576
  (6 shorter events, 0.0 us)
where the time goes:
time: 51.8 us; the launch traced here: 51.4 us
  Pallas kernels  45.2 us (87%)
  local copies, waits for them, and re-layouts  3.41 us (7%)
  other arithmetic  2.2 us (4%)
  between operations  0.68 us (1%)
    pallas_call x1, Pallas kernels, per_device(): pl.pallas_call(kernel, out_shape=(jax.ShapeDtypeStruct((16, 32, 256), F32...  45.2 us
    unnamed x1, local copies, waits for them, and re-layouts  1.88 us
    pallas_call x1, local copies, waits for them, and re-layouts, per_device(): pl.pallas_call(kernel, out_shape=(jax.ShapeDtypeStruct((16, 32, 256), F32...  1.53 us
    convert_element_type x2, other arithmetic, sums(): return jnp.where(k // 2 == c, 1.0, 0.0).astype(BF16)  1.45 us

commit v1 on v0

--- a/solution.py
+++ b/solution.py
@@ -20,9 +20,9 @@
 LANES = (256, 128, 128, 128)
 
 NEAR = [(a, b) for a in (-1, 0, 1) for b in (-1, 0, 1) if (a, b) != (0, 0)]
-WIDE = [(a, b) for a in range(-3, 4) for b in (-1, 0, 1) if (a, b) != (0, 0)]
-ALONG = [(0, k) for k in range(1, NL)]
-GREET = [(a, b % NL) for a, b in WIDE] + [(0, k) for k in range(2, NL - 1)]
+WIDE = [(a, b) for c in (3, 2, 1, 0) for a in (-c, c)[:1 + (c > 0)] for b in (-1, 1, 0) if (a, b) != (0, 0)]
+ALONG = [(0, k) for k in (10, 9, 11, 6, 5, 7, 14, 13, 2, 8, 3, 15, 12, 4, 1)]
+GREET = [to for to in WIDE if to[0]] + ALONG
 
 
 def lane_ids(shape):
@@ -183,12 +183,13 @@
 
 
 def kernel(*refs):
-    (rhs, phase, r0_mat, r1_mat, r2_mat, p0_mat, p1_mat, fine_out, coarse_out) = refs[:9]
-    refs = refs[9:]
+    rhs, phase, fine_out, coarse_out = refs[:4]
+    refs = refs[4:]
     windows = [refs[9 * k:9 * k + 9] for k in range(4)]
     (
         ph, upk, dpk, rxl0, rxh0, rs, s0, out, ct1, n1, h0,
         rxl1, rxh1, crl1, crh1, c1w, s1, ct2, pf2, pn2, rf2, rn2, n2w, n3s, s2, pf3, pc3, rf3, rc3,
+        r0_mat, r1_mat, r2_mat, p0_mat, p1_mat,
         lsem, ss0, rs0, sf1, qf1, sc1, qc1, sf2, qf2, sc2, qc2, sf3, qf3, sc3, qc3,
     ) = refs[36:]
     g = lax.axis_index("grp")
@@ -200,49 +201,80 @@
     def device(dg, dl):
         return lax.rem(g + dg + NG, NG), lax.rem(l + dl + NL, NL)
 
-    def send(src, dst, s_sem, r_sem, to):
-        copy = pltpu.make_async_remote_copy(
-            src_ref=src, dst_ref=dst, send_sem=s_sem, recv_sem=r_sem,
-            device_id=device(*to), device_id_type=MESH,
-        )
-        copy.start()
-        sent.append(copy)
-        return copy
+    def inside(dg, dl):
+        tests = [t for t in (
+            g + dg >= 0 if dg < 0 else None, g + dg < NG if dg > 0 else None,
+            l + dl >= 0 if dl < 0 else None, l + dl < NL if dl > 0 else None,
+        ) if t is not None]
+        return functools.reduce(jnp.logical_and, tests)
+
+    def run(test, action):
+        action() if test is None else pl.when(test)(action)
+
+    class Sent:
+        def __init__(self, src, dst, s_sem, r_sem, to, wrap):
+            self.copy = pltpu.make_async_remote_copy(
+                src_ref=src, dst_ref=dst, send_sem=s_sem, recv_sem=r_sem,
+                device_id=device(*to), device_id_type=MESH,
+            )
+            self.out = None if wrap else inside(*to)
+            self.back = None if wrap else inside(-to[0], -to[1])
+            run(self.out, self.copy.start)
+            sent.append(self)
+
+        def wait_recv(self):
+            run(self.back, self.copy.wait_recv)
+
+        def wait_send(self):
+            run(self.out, self.copy.wait_send)
+
+    def send(src, dst, s_sem, r_sem, to, wrap=False):
+        return Sent(src, dst, s_sem, r_sem, to, wrap)
 
     load_f = pltpu.make_async_copy(rhs, L0.F.at[4:20, 0:32], lsem.at[0])
     load_p = pltpu.make_async_copy(phase, ph, lsem.at[1])
     load_p.start()
     load_f.start()
     barrier = pltpu.get_barrier_semaphore()
+    expected = jnp.int32(0)
     for to in GREET:
-        pl.semaphore_signal(barrier, inc=1, device_id=device(*to), device_id_type=MESH)
+        test = inside(*to) if to[0] or to[1] < 0 else None
+
+        def greet(to=to):
+            pl.semaphore_signal(barrier, inc=1, device_id=device(*to), device_id_type=MESH)
+
+        run(test, greet)
+        expected = expected + (1 if test is None else jnp.where(test, 1, 0))
+
+    def clear(test, *refs):
+        @pl.when(test)
+        def _():
+            for ref in refs:
+                ref[...] = jnp.zeros(ref.shape, F32)
+
+    near_tiles = (rxl1, rxh1, crl1, crh1)
+    clear(
+        g == 0, L0.F.at[0:4, 0:32], L0.C.at[0:4, 0:32], L1.F.at[0:4, 0:16], L1.C.at[0:4, 0:16],
+        *[x.at[0:4] for x in (rxl0, rxh0) + near_tiles],
+    )
+    clear(
+        g == NG - 1, L0.F.at[20:22, 0:32], L0.C.at[20:22, 0:32], L1.F.at[12:14, 0:16], L1.C.at[12:14, 0:16],
+        *[x.at[20:22] for x in (rxl0, rxh0)], *[x.at[12:14] for x in near_tiles],
+    )
+    clear(l == 0, rxl0, rxl1, crl1, rf2.at[:, 0], rn2.at[:, 0])
+    clear(l == NL - 1, rxh0, rxh1, crh1, rf2.at[:, 2], rn2.at[:, 2])
+    for d in (1, 2, 3):
+        clear(g < d, rf2.at[3 - d], rn2.at[3 - d])
+        clear(g >= NG - d, rf2.at[3 + d], rn2.at[3 + d])
 
     load_p.wait()
     gas = ph[...].astype(F32)
     L0.C[4:20, 0:32] = 1.0 + 999.0 * gas
-    pairs = jnp.concatenate([gas[2 * i:2 * i + 1] + gas[2 * i + 1:2 * i + 2] for i in range(8)], 0)
-    ct1[...] = jnp.dot(
-        pairs.reshape(8 * 32, 256).astype(BF16), p0_mat[...], preferred_element_type=F32
-    ).reshape(8, 32, 128)
-    n1[...] = ct1[:, pl.ds(0, 16, stride=2), :] + ct1[:, pl.ds(1, 16, stride=2), :]
-    count1 = n1[...]
-    L1.C[4:12, 0:16] = 1.0 + 124.875 * count1
-    pairs = jnp.concatenate([count1[2 * i:2 * i + 1] + count1[2 * i + 1:2 * i + 2] for i in range(4)], 0)
-    ct2[...] = jnp.dot(
-        pairs.reshape(4 * 16, 128).astype(BF16), p1_mat[...], preferred_element_type=F32
-    ).reshape(4, 16, 128)
-    count2 = ct2[:, pl.ds(0, 8, stride=2), :] + ct2[:, pl.ds(1, 8, stride=2), :]
-    pn2[...] = count2[0:2] + pltpu.roll(count2[2:4], 64, 2)
-    rn2[3, 1] = pn2[...]
-
     load_f.wait()
     sub = row_ids((1, 8, 256)) < 4
     upk[...] = jnp.where(sub, pltpu.roll(L0.C[4:20, 24:32], 4, 1), L0.F[4:20, 24:32])
     dpk[...] = jnp.where(sub, L0.F[4:20, 0:8], pltpu.roll(L0.C[4:20, 0:8], 4, 1))
-    for ref in (L3.F, L3.C):
-        ref[:, 64:72] = jnp.zeros((PLANES[3], 8, 128), F32)
-
-    pl.semaphore_wait(barrier, len(GREET))
+    pl.semaphore_wait(barrier, expected)
 
     first = []
     k = 0
@@ -279,7 +311,37 @@
 
     def along_sends(src, slots, ssem, rsem):
         mine = slots.at[lax.div(l, 2), lax.rem(l, 2)]
-        return [send(src, mine, ssem.at[k], rsem.at[k], to) for k, to in enumerate(ALONG)]
+        return [send(src, mine, ssem.at[k], rsem.at[k], to, True) for k, to in enumerate(ALONG)]
+
+    weights = ((r0_mat, 256), (r1_mat, 128), (r2_mat, 64))
+    for ref, used in weights:
+        k, c = row_ids(ref.shape), lane_ids(ref.shape)
+        near = jnp.abs(k - 2 * c)
+        live = (k < used) & (c < used // 2)
+        ref[...] = jnp.where(
+            live & (near == 0), 0.5, jnp.where(live & (near == 1), 0.25, 0.0)
+        ).astype(BF16)
+    for ref in (p0_mat, p1_mat):
+        half = row_ids(ref.shape) - 2 * lane_ids(ref.shape)
+        ref[...] = jnp.where((half == 0) | (half == 1), 1.0, 0.0).astype(BF16)
+
+    pairs = jnp.concatenate([gas[2 * i:2 * i + 1] + gas[2 * i + 1:2 * i + 2] for i in range(8)], 0)
+    ct1[...] = jnp.dot(
+        pairs.reshape(8 * 32, 256).astype(BF16), p0_mat[...], preferred_element_type=F32
+    ).reshape(8, 32, 128)
+    n1[...] = ct1[:, pl.ds(0, 16, stride=2), :] + ct1[:, pl.ds(1, 16, stride=2), :]
+    count1 = n1[...]
+    L1.C[4:12, 0:16] = 1.0 + 124.875 * count1
+    pairs = jnp.concatenate([count1[2 * i:2 * i + 1] + count1[2 * i + 1:2 * i + 2] for i in range(4)], 0)
+    ct2[...] = jnp.dot(
+        pairs.reshape(4 * 16, 128).astype(BF16), p1_mat[...], preferred_element_type=F32
+    ).reshape(4, 16, 128)
+    count2 = ct2[:, pl.ds(0, 8, stride=2), :] + ct2[:, pl.ds(1, 8, stride=2), :]
+    pn2[...] = count2[0:2] + pltpu.roll(count2[2:4], 64, 2)
+    rn2[3, 1] = pn2[...]
+
+    for ref in (L3.F, L3.C):
+        ref[:, 64:72] = jnp.zeros((PLANES[3], 8, 128), F32)
 
     got_c1 = near_sends(L1.C, crl1, crh1, sc1, qc1, 4)
     got_c2 = wide_sends(pn2, rn2, sc2, qc2)
@@ -459,28 +521,13 @@
     for sweep in range(COARSE_SWEEPS - 1):
         L3.sweep_all(source, target, 2 + sweep, 10 - sweep)
         source, target = target, source
-    coarse_out[...] = ((8.0 / 12.0) * L3.residual_all(source, 5, 7))[:, 0:64, 0:32]
+    last = (8.0 / 12.0) * L3.residual_all(source, 5, 7)
+    for i in range(2):
+        coarse_out[i] = jnp.transpose(last[i, 0:64], (1, 0))[0:32]
 
     store.wait()
     for copy in sent:
         copy.wait_send()
-
-
-def lane_matrices():
-    def weights(size, used):
-        k = jnp.arange(size)[:, None]
-        c = jnp.arange(128)[None, :]
-        live = (k < used) & (c < used // 2)
-        near = jnp.abs(k - 2 * c)
-        full = jnp.where(live, jnp.where(near == 0, 0.5, jnp.where(near == 1, 0.25, 0.0)), 0.0)
-        return full.astype(BF16)
-
-    def sums(size):
-        k = jnp.arange(size)[:, None]
-        c = jnp.arange(128)[None, :]
-        return jnp.where(k // 2 == c, 1.0, 0.0).astype(BF16)
-
-    return weights(256, 256), weights(128, 128), weights(128, 64), sums(256), sums(128)
 
 
 def per_device(right_side, phase):
@@ -506,6 +553,8 @@
             ((28, 16, 128), F32), ((11, 8, 128), F32), ((21, 16, 128), F32),
             ((2, 8, 128), F32), ((2, 8, 128), F32),
             ((8, 2, 2, 8, 128), F32), ((8, 2, 2, 8, 128), F32),
+            ((256, 128), BF16), ((128, 128), BF16), ((128, 128), BF16),
+            ((256, 128), BF16), ((128, 128), BF16),
         )
     ]
     scratch.append(pltpu.SemaphoreType.DMA((3,)))
@@ -513,19 +562,20 @@
         scratch += [pltpu.SemaphoreType.DMA((n,)), pltpu.SemaphoreType.DMA((n,))]
     vmem = pl.BlockSpec(memory_space=pltpu.VMEM)
     hbm = pl.BlockSpec(memory_space=pl.ANY)
-    return pl.pallas_call(
+    fine, coarse = pl.pallas_call(
         kernel,
         out_shape=(
             jax.ShapeDtypeStruct((16, 32, 256), F32),
-            jax.ShapeDtypeStruct((2, 64, 32), F32),
+            jax.ShapeDtypeStruct((2, 32, 64), F32),
         ),
-        in_specs=[hbm, hbm] + [vmem] * 5,
+        in_specs=[hbm, hbm],
         out_specs=(hbm, vmem),
         scratch_shapes=scratch,
         compiler_params=pltpu.CompilerParams(
             collective_id=0, has_side_effects=True, vmem_limit_bytes=56 * 2**20
         ),
-    )(right_side, phase, *lane_matrices())
+    )(right_side, phase)
+    return fine, jnp.transpose(coarse, (0, 2, 1))
 
 
 def solution(mesh):

time: 51.8 us -> 44.3 us (0.86)
  Pallas kernels: 45.2 us -> 41 us
  other arithmetic: 2.2 us -> 0 us
  local copies, waits for them, and re-layouts: 3.41 us -> 2.51 us
    pallas_call x1, Pallas kernels: 45.2 us -> 41 us  [per_device(): pl.pallas_call(kernel, out_shape=(jax.ShapeDtypeStruct((16, 32, 256), F32...]
    convert_element_type x3 -> x0, other arithmetic: 2.17 us -> none  [the longest x2 1.45 us: sums(): return jnp.where(k // 2 == c, 1.0, 0.0).astype(BF16)]
    pallas_call x1 -> x0, local copies, waits for them, and re-layouts: 1.53 us -> none  [per_device(): pl.pallas_call(kernel, out_shape=(jax.ShapeDtypeStruct((16, 32, 256), F32...]
    unnamed x1 -> x4, local copies, waits for them, and re-layouts: 1.88 us -> 2.51 us
where the time goes in v1:
time: 44.3 us; the launch traced here: 44.1 us
  Pallas kernels  41 us (93%)
  local copies, waits for them, and re-layouts  2.51 us (6%)
  between operations  0.65 us (1%)
    pallas_call x1, Pallas kernels, per_device(): pl.pallas_call(kernel, out_shape=(jax.ShapeDtypeStruct((16, 32, 256), F32...  41 us
    unnamed x4, local copies, waits for them, and re-layouts  2.51 us

profile of v1, /device:TPU:1, one launch (start us, length us, event | category | flops | bytes accessed | tf_op | source)
XLA Modules:
  0.0 44.1 jit_solution(7160418642196779350)
XLA Ops:
  0.6 41.0 %shard_map.41 = (f32[16,32,256]{2,1,0:T(8,128)}, f32[2,32,64]{2,1,0:T(8,128)}) custom-call(f32[16,32,256]{2,1,0:T(8,128)} %refs_0_.1, s32[16,32,256]{2,1,0:T(8,128)} %refs_1_.1), custom_call_target="tpu_custom_call" | custom-call | tf_op jit(solution)/shard_map/pallas_call | solution.py:565
  41.6 0.0 copy-start
  41.6 1.9 %copy.6 = f32[16,32,256]{2,1,0:T(8,128)} copy(f32[16,32,256]{2,1,0:T(8,128)} %get-tuple-element.8) | data formatting | bytes 1048576
  43.5 0.0 copy-done
  43.5 0.6 %copy.7 = f32[2,64,32]{1,2,0:T(8,128)} copy(f32[2,64,32]{1,2,0:T(8,128)S(1)} %bitcast.1) | data formatting | bytes 32768
Async XLA Ops:
  41.6 1.9 %copy-start = (f32[2,32,64]{2,1,0:T(8,128)S(1)}, f32[2,32,64]{2,1,0:T(8,128)}, u32[]{:S(2)}) copy-start(f32[2,32,64]{2,1,0:T(8,128)} %get-tuple-element.5) | copy-start | bytes 49156

commit v2 on v1

--- a/solution.py
+++ b/solution.py
@@ -346,8 +346,6 @@
     got_c1 = near_sends(L1.C, crl1, crh1, sc1, qc1, 4)
     got_c2 = wide_sends(pn2, rn2, sc2, qc2)
 
-    for copy in first:
-        copy.wait_recv()
     rows0 = L0.row_valid((40, 256))
     sub = row_ids((8, 256)) < 4
 
@@ -356,10 +354,6 @@
         L0.F[i, 32:40] = jnp.where(sub, high, low)
         L0.C[i, 32:40] = pltpu.roll(jnp.where(sub, low, high), 4, 0) * rows0[32:40] * L0.plane_valid(i)
         return 0
-
-    lax.fori_loop(0, 22, merge, 0)
-    for i in (0, 1, 2, 3, 20, 21):
-        L0.C[i, 0:32] = L0.C[i, 0:32] * L0.plane_valid(i)
 
     def setup(i, before):
         cells = L0.cells(L0.C[i])
@@ -368,37 +362,56 @@
         L0.U[i] = w * (12.0 * L0.F[i])
         return cells
 
-    before = L0.cells(L0.C[0])
-    L0.Ei[0] = before[2]
-    L0.planes_loop(1, 22, setup, before, 3)
-
     def second(i, u, b):
         L0.V[i] = u + L0.W[i] * (12.0 * L0.F[i] - b)
 
-    L0.apply_loop(L0.U, 2, 21, second, 3)
-
     def residual(i, u, b):
         r = (12.0 * L0.F[i] - b) * (rows0 * L0.plane_valid(i))
-        rs[i - 3, 0:8] = r[32:40]
-        rs[i - 3, 8:40] = r[0:32]
+        for half in range(2):
+            lanes = slice(128 * half, 128 * half + 128)
+            rs[i - 3, half, 0:8] = r[32:40, lanes]
+            rs[i - 3, half, 8:40] = r[0:32, lanes]
         out[jnp.maximum(i - 4, 0)] = r[0:32] * (1.0 / 12.0)
 
+    def setup_planes(lo, hi):
+        before = L0.cells(L0.C[lo - 1])
+        L0.Ei[lo - 1] = before[2]
+        L0.planes_loop(lo, hi, setup, before, 3)
+
+    for copy in first[:2]:
+        copy.wait_recv()
+    lax.fori_loop(4, 20, merge, 0)
+    setup_planes(5, 20)
+    L0.apply_loop(L0.U, 6, 19, second, 3)
+    for copy in first[2:]:
+        copy.wait_recv()
+    for i in (0, 1, 2, 3, 20, 21):
+        merge(i, 0)
+        L0.C[i, 0:32] = L0.C[i, 0:32] * L0.plane_valid(i)
+    setup_planes(1, 5)
+    setup_planes(20, 22)
+    L0.apply_loop(L0.U, 2, 6, second, 4)
+    L0.apply_loop(L0.U, 19, 21, second, 2)
     L0.apply_loop(L0.V, 3, 20, residual, 3)
     store = pltpu.make_async_copy(out, fine_out, lsem.at[2])
     store.start()
 
-    def restrict(scratch, matrix, planes, rows, lanes, kept):
-        scratch_r, scratch_s = scratch
-        scratch_s[...] = split_dot(scratch_r.reshape(planes * rows, lanes), matrix).reshape(planes, rows, 128)
-        h = 0.5 * (
-            scratch_s[:, pl.ds(7, kept, stride=2), :] + scratch_s[:, pl.ds(9, kept, stride=2), :]
-        ) + scratch_s[:, pl.ds(8, kept, stride=2), :]
-        count = (planes - 1) // 2
-        return [0.5 * (h[2 * i] + h[2 * i + 2]) + h[2 * i + 1] for i in range(count)]
-
-    f1 = restrict((rs[...], s0), r0_mat[...], 17, 40, 256, 16)
-    for i in range(8):
-        L1.F[4 + i, 0:16] = f1[i]
+    def coarser_planes(r):
+        return [0.5 * (r[2 * i] + r[2 * i + 2]) + r[2 * i + 1] for i in range((r.shape[0] - 1) // 2)]
+
+    def coarser_rows(ref, kept):
+        return 0.5 * (
+            ref[:, pl.ds(7, kept, stride=2), :] + ref[:, pl.ds(9, kept, stride=2), :]
+        ) + ref[:, pl.ds(8, kept, stride=2), :]
+
+    total = jnp.zeros((8 * 16, 128), F32)
+    for half in range(2):
+        for i, plane in enumerate(coarser_planes(rs[:, half])):
+            s0[half, i] = plane
+        total = total + split_dot(
+            coarser_rows(s0.at[half], 16).reshape(8 * 16, 128), r0_mat[128 * half:128 * half + 128]
+        )
+    L1.F[4:12, 0:16] = total.reshape(8, 16, 128)
     got_f1 = near_sends(L1.F, rxl1, rxh1, sf1, qf1, 3)
 
     for copy in got_c1:
@@ -476,10 +489,10 @@
     L1.sweep_all(L1.U, L1.V, 2, 13)
     r1 = L1.residual_all(L1.V, 3, 12) * valid1[3:12]
     r1 = jnp.concatenate([r1[:, 16:24], r1[:, 0:16]], 1)
-    f2 = restrict((r1, s1), r1_mat[...], 9, 24, 128, 8)
-    pf2[...] = jnp.concatenate([x[None] for x in f2[0:2]], 0) + pltpu.roll(
-        jnp.concatenate([x[None] for x in f2[2:4]], 0), 64, 2
-    )
+    for i, plane in enumerate(coarser_planes(r1)):
+        s1[i] = plane
+    f2 = split_dot(coarser_rows(s1, 8).reshape(4 * 8, 128), r1_mat[...]).reshape(4, 8, 128)
+    pf2[...] = f2[0:2] + pltpu.roll(f2[2:4], 64, 2)
     rf2[3, 1] = pf2[...]
     got_f2 = wide_sends(pf2, rf2, sf2, qf2)
 
@@ -504,9 +517,11 @@
     L2.first_all(1, 26)
     L2.sweep_all(L2.U, L2.V, 2, 25)
     r2 = L2.residual_all(L2.V, 3, 24) * valid2[3:24]
-    r2 = jnp.concatenate([r2[:, 8:16], r2[:, 0:8]], 1)
-    f3 = restrict((r2, s2), r2_mat[...], 21, 16, 128, 4)
-    pack(f3, pf3)
+    for i, plane in enumerate(coarser_planes(r2)):
+        s2[i, 0:8] = plane[8:16]
+        s2[i, 8:24] = plane
+    f3 = split_dot(coarser_rows(s2, 8).reshape(10 * 8, 128), r2_mat[...]).reshape(10, 8, 128)
+    pack([f3[i, 0:4] for i in range(10)], pf3)
     rf3[lax.div(l, 2), lax.rem(l, 2)] = pf3[...]
     got_f3 = along_sends(pf3, rf3, sf3, qf3)
     for copy in got_f3:
@@ -541,16 +556,16 @@
             ((16, 32, 256), jnp.int32),
             ((16, 8, 256), F32), ((16, 8, 256), F32),
             ((22, 8, 256), F32), ((22, 8, 256), F32),
-            ((17, 40, 256), F32), ((17, 40, 128), F32),
+            ((17, 2, 40, 128), F32), ((2, 8, 40, 128), F32),
             ((16, 32, 256), F32),
             ((8, 32, 128), F32), ((8, 16, 128), F32), ((17, 16, 128), F32),
             ((14, 8, 128), F32), ((14, 8, 128), F32), ((14, 8, 128), F32), ((14, 8, 128), F32),
             ((14, 24, 128), F32),
-            ((9, 24, 128), F32),
+            ((4, 24, 128), F32),
             ((4, 16, 128), F32),
             ((2, 8, 128), F32), ((2, 8, 128), F32),
             ((7, 3, 2, 8, 128), F32), ((7, 3, 2, 8, 128), F32),
-            ((28, 16, 128), F32), ((11, 8, 128), F32), ((21, 16, 128), F32),
+            ((28, 16, 128), F32), ((11, 8, 128), F32), ((10, 24, 128), F32),
             ((2, 8, 128), F32), ((2, 8, 128), F32),
             ((8, 2, 2, 8, 128), F32), ((8, 2, 2, 8, 128), F32),
             ((256, 128), BF16), ((128, 128), BF16), ((128, 128), BF16),
@@ -572,9 +587,9 @@
         out_specs=(hbm, vmem),
         scratch_shapes=scratch,
         compiler_params=pltpu.CompilerParams(
-            collective_id=0, has_side_effects=True, vmem_limit_bytes=56 * 2**20
+            collective_id=0, has_side_effects=True, vmem_limit_bytes=24 * 2**20
         ),
-    )(right_side, phase)
+    )(pltpu.with_memory_space_constraint(right_side, pltpu.HBM), pltpu.with_memory_space_constraint(phase, pltpu.HBM))
     return fine, jnp.transpose(coarse, (0, 2, 1))
 
 

time: 44.3 us -> 40.8 us (0.921)
  Pallas kernels: 41 us -> 38.1 us
  local copies, waits for them, and re-layouts: 2.51 us -> 1.41 us
    pallas_call x1, Pallas kernels: 41 us -> 38.1 us  [per_device(): pl.pallas_call(kernel, out_shape=(jax.ShapeDtypeStruct((16, 32, 256), F32...]
    unnamed x4 -> x2, local copies, waits for them, and re-layouts: 2.51 us -> 1.41 us
where the time goes in v2:
time: 40.8 us; the launch traced here: 40.2 us
  Pallas kernels  38.1 us (93%)
  local copies, waits for them, and re-layouts  1.41 us (3%)
  between operations  0.64 us (2%)
    pallas_call x1, Pallas kernels, per_device(): pl.pallas_call(kernel, out_shape=(jax.ShapeDtypeStruct((16, 32, 256), F32...  38.1 us
    unnamed x2, local copies, waits for them, and re-layouts  1.41 us

profile of v2, /device:TPU:1, one launch (start us, length us, event | category | flops | bytes accessed | tf_op | source)
XLA Modules:
  0.0 40.2 jit_solution(15600374718413351114)
XLA Ops:
  0.6 38.1 %shard_map.41 = (f32[16,32,256]{2,1,0:T(8,128)S(1)}, f32[2,32,64]{2,1,0:T(8,128)S(1)}) custom-call(f32[16,32,256]{2,1,0:T(8,128)} %refs_0_.1, s32[16,32,256]{2,1,0:T(8,128)} %refs_1_.1), custom_call_target="tpu_custom_call" | custom-call | tf_op jit(solution)/shard_map/pallas_call | solution.py:580
  38.8 0.8 %copy.6 = f32[16,32,256]{2,1,0:T(8,128)} copy(f32[16,32,256]{2,1,0:T(8,128)S(1)} %get-tuple-element.8) | data formatting | bytes 1048576
  39.6 0.6 %copy.7 = f32[2,64,32]{1,2,0:T(8,128)} copy(f32[2,64,32]{1,2,0:T(8,128)S(1)} %bitcast.1) | data formatting | bytes 32768

commit v3 on v2

--- a/solution.py
+++ b/solution.py
@@ -22,7 +22,6 @@
 NEAR = [(a, b) for a in (-1, 0, 1) for b in (-1, 0, 1) if (a, b) != (0, 0)]
 WIDE = [(a, b) for c in (3, 2, 1, 0) for a in (-c, c)[:1 + (c > 0)] for b in (-1, 1, 0) if (a, b) != (0, 0)]
 ALONG = [(0, k) for k in (10, 9, 11, 6, 5, 7, 14, 13, 2, 8, 3, 15, 12, 4, 1)]
-GREET = [to for to in WIDE if to[0]] + ALONG
 
 
 def lane_ids(shape):
@@ -190,7 +189,7 @@
         ph, upk, dpk, rxl0, rxh0, rs, s0, out, ct1, n1, h0,
         rxl1, rxh1, crl1, crh1, c1w, s1, ct2, pf2, pn2, rf2, rn2, n2w, n3s, s2, pf3, pc3, rf3, rc3,
         r0_mat, r1_mat, r2_mat, p0_mat, p1_mat,
-        lsem, ss0, rs0, sf1, qf1, sc1, qc1, sf2, qf2, sc2, qc2, sf3, qf3, sc3, qc3,
+        lsem, known, ss0, rs0, sf1, qf1, sc1, qc1, sf2, qf2, sc2, qc2, sf3, qf3, sc3, qc3,
     ) = refs[36:]
     g = lax.axis_index("grp")
     l = lax.axis_index("loc")
@@ -236,15 +235,19 @@
     load_p.start()
     load_f.start()
     barrier = pltpu.get_barrier_semaphore()
-    expected = jnp.int32(0)
-    for to in GREET:
-        test = inside(*to) if to[0] or to[1] < 0 else None
-
-        def greet(to=to):
-            pl.semaphore_signal(barrier, inc=1, device_id=device(*to), device_id_type=MESH)
-
-        run(test, greet)
-        expected = expected + (1 if test is None else jnp.where(test, 1, 0))
+    def greet(sem, targets):
+        count = jnp.int32(0)
+        for to in targets:
+            test = inside(*to)
+
+            def signal(to=to):
+                pl.semaphore_signal(sem, inc=1, device_id=device(*to), device_id_type=MESH)
+
+            run(test, signal)
+            count = count + jnp.where(test, 1, 0)
+        return count
+
+    around = greet(barrier, NEAR)
 
     def clear(test, *refs):
         @pl.when(test)
@@ -274,13 +277,15 @@
     sub = row_ids((1, 8, 256)) < 4
     upk[...] = jnp.where(sub, pltpu.roll(L0.C[4:20, 24:32], 4, 1), L0.F[4:20, 24:32])
     dpk[...] = jnp.where(sub, L0.F[4:20, 0:8], pltpu.roll(L0.C[4:20, 0:8], 4, 1))
-    pl.semaphore_wait(barrier, expected)
+    pl.semaphore_wait(barrier, around)
 
     first = []
     k = 0
     for src, dst, to in (
-        (upk, rxl0.at[4:20], (0, 1)),
-        (dpk, rxh0.at[4:20], (0, -1)),
+        (upk.at[0:8], rxl0.at[4:12], (0, 1)),
+        (dpk.at[0:8], rxh0.at[4:12], (0, -1)),
+        (upk.at[8:16], rxl0.at[12:20], (0, 1)),
+        (dpk.at[8:16], rxh0.at[12:20], (0, -1)),
         (L0.C.at[16:20, 0:32], L0.C.at[0:4, 0:32], (1, 0)),
         (L0.F.at[17:20, 0:32], L0.F.at[1:4, 0:32], (1, 0)),
         (L0.C.at[4:6, 0:32], L0.C.at[20:22, 0:32], (-1, 0)),
@@ -312,6 +317,8 @@
     def along_sends(src, slots, ssem, rsem):
         mine = slots.at[lax.div(l, 2), lax.rem(l, 2)]
         return [send(src, mine, ssem.at[k], rsem.at[k], to, True) for k, to in enumerate(ALONG)]
+
+    greet(known.at[0], NEAR)
 
     weights = ((r0_mat, 256), (r1_mat, 128), (r2_mat, 64))
     for ref, used in weights:
@@ -344,7 +351,9 @@
         ref[:, 64:72] = jnp.zeros((PLANES[3], 8, 128), F32)
 
     got_c1 = near_sends(L1.C, crl1, crh1, sc1, qc1, 4)
-    got_c2 = wide_sends(pn2, rn2, sc2, qc2)
+    pl.semaphore_wait(known.at[0], around)
+    known_1 = greet(known.at[1], [(-1, 0), (1, 0)])
+    known_2 = greet(known.at[2], [(0, -2), (0, 2)])
 
     rows0 = L0.row_valid((40, 256))
     sub = row_ids((8, 256)) < 4
@@ -376,14 +385,20 @@
     def setup_planes(lo, hi):
         before = L0.cells(L0.C[lo - 1])
         L0.Ei[lo - 1] = before[2]
-        L0.planes_loop(lo, hi, setup, before, 3)
+        L0.planes_loop(lo, hi, setup, before, 8)
 
     for copy in first[:2]:
         copy.wait_recv()
-    lax.fori_loop(4, 20, merge, 0)
-    setup_planes(5, 20)
-    L0.apply_loop(L0.U, 6, 19, second, 3)
-    for copy in first[2:]:
+    lax.fori_loop(4, 12, merge, 0)
+    setup_planes(5, 12)
+    L0.apply_loop(L0.U, 6, 11, second, 6)
+    for copy in first[2:4]:
+        copy.wait_recv()
+    lax.fori_loop(12, 20, merge, 0)
+    setup_planes(12, 20)
+    L0.apply_loop(L0.U, 11, 19, second, 4)
+    L0.apply_loop(L0.V, 7, 18, residual, 6)
+    for copy in first[4:]:
         copy.wait_recv()
     for i in (0, 1, 2, 3, 20, 21):
         merge(i, 0)
@@ -391,8 +406,9 @@
     setup_planes(1, 5)
     setup_planes(20, 22)
     L0.apply_loop(L0.U, 2, 6, second, 4)
-    L0.apply_loop(L0.U, 19, 21, second, 2)
-    L0.apply_loop(L0.V, 3, 20, residual, 3)
+    L0.apply_loop(L0.U, 19, 21, second, 4)
+    L0.apply_loop(L0.V, 3, 7, residual, 4)
+    L0.apply_loop(L0.V, 18, 20, residual, 4)
     store = pltpu.make_async_copy(out, fine_out, lsem.at[2])
     store.start()
 
@@ -414,6 +430,11 @@
     L1.F[4:12, 0:16] = total.reshape(8, 16, 128)
     got_f1 = near_sends(L1.F, rxl1, rxh1, sf1, qf1, 3)
 
+    pl.semaphore_wait(known.at[1], known_1)
+    pl.semaphore_wait(known.at[2], known_2)
+    known_3 = greet(known.at[3], [(0, -4), (0, 4)])
+    got_c2 = wide_sends(pn2, rn2, sc2, qc2)
+
     for copy in got_c1:
         copy.wait_recv()
     sub1 = row_ids((1, 8, 128)) < 4
@@ -422,6 +443,25 @@
     c1w[:, 16:24] = jnp.where(sub1, crh1[...], crl1[...]) * valid1[:, 16:24]
     L1.C = c1w
     L1.setup_all(1, 14)
+
+    pl.semaphore_wait(known.at[3], known_3)
+    known_4 = greet(known.at[4], [(0, -8), (0, 8)])
+
+    for copy in got_f1:
+        copy.wait_recv()
+    L1.F[1:14, 16:24] = jnp.where(sub1, rxh1[1:14], rxl1[1:14])
+    L1.first_all(1, 14)
+    L1.sweep_all(L1.U, L1.V, 2, 13)
+    r1 = L1.residual_all(L1.V, 3, 12) * valid1[3:12]
+    r1 = jnp.concatenate([r1[:, 16:24], r1[:, 0:16]], 1)
+    for i, plane in enumerate(coarser_planes(r1)):
+        s1[i] = plane
+    f2 = split_dot(coarser_rows(s1, 8).reshape(4 * 8, 128), r1_mat[...]).reshape(4, 8, 128)
+    pf2[...] = f2[0:2] + pltpu.roll(f2[2:4], 64, 2)
+    rf2[3, 1] = pf2[...]
+    got_f2 = wide_sends(pf2, rf2, sf2, qf2)
+
+    pl.semaphore_wait(known.at[4], known_4)
 
     def unpack_wide(slots, put):
         lane = lane_ids((1, 1, 1, 128)) < 64
@@ -482,31 +522,6 @@
     rc3[lax.div(l, 2), lax.rem(l, 2)] = pc3[...]
     got_c3 = along_sends(pc3, rc3, sc3, qc3)
 
-    for copy in got_f1:
-        copy.wait_recv()
-    L1.F[1:14, 16:24] = jnp.where(sub1, rxh1[1:14], rxl1[1:14])
-    L1.first_all(1, 14)
-    L1.sweep_all(L1.U, L1.V, 2, 13)
-    r1 = L1.residual_all(L1.V, 3, 12) * valid1[3:12]
-    r1 = jnp.concatenate([r1[:, 16:24], r1[:, 0:16]], 1)
-    for i, plane in enumerate(coarser_planes(r1)):
-        s1[i] = plane
-    f2 = split_dot(coarser_rows(s1, 8).reshape(4 * 8, 128), r1_mat[...]).reshape(4, 8, 128)
-    pf2[...] = f2[0:2] + pltpu.roll(f2[2:4], 64, 2)
-    rf2[3, 1] = pf2[...]
-    got_f2 = wide_sends(pf2, rf2, sf2, qf2)
-
-    for copy in got_c3:
-        copy.wait_recv()
-
-    def put_c3(p, value):
-        L3.C[p, 0:64] = (1.0 + (999.0 / 512.0) * value) * (
-            L3.row_valid((72, 128))[0:64] * L3.plane_valid(p)
-        )
-
-    unpack_along(rc3, 11, put_c3)
-    L3.setup_all(1, 11)
-
     for copy in got_f2:
         copy.wait_recv()
 
@@ -524,6 +539,18 @@
     pack([f3[i, 0:4] for i in range(10)], pf3)
     rf3[lax.div(l, 2), lax.rem(l, 2)] = pf3[...]
     got_f3 = along_sends(pf3, rf3, sf3, qf3)
+
+    for copy in got_c3:
+        copy.wait_recv()
+
+    def put_c3(p, value):
+        L3.C[p, 0:64] = (1.0 + (999.0 / 512.0) * value) * (
+            L3.row_valid((72, 128))[0:64] * L3.plane_valid(p)
+        )
+
+    unpack_along(rc3, 11, put_c3)
+    L3.setup_all(1, 11)
+
     for copy in got_f3:
         copy.wait_recv()
 
@@ -572,8 +599,8 @@
             ((256, 128), BF16), ((128, 128), BF16),
         )
     ]
-    scratch.append(pltpu.SemaphoreType.DMA((3,)))
-    for n in (10, len(NEAR), len(NEAR), len(WIDE), len(WIDE), len(ALONG), len(ALONG)):
+    scratch += [pltpu.SemaphoreType.DMA((3,)), pltpu.SemaphoreType.REGULAR((5,))]
+    for n in (12, len(NEAR), len(NEAR), len(WIDE), len(WIDE), len(ALONG), len(ALONG)):
         scratch += [pltpu.SemaphoreType.DMA((n,)), pltpu.SemaphoreType.DMA((n,))]
     vmem = pl.BlockSpec(memory_space=pltpu.VMEM)
     hbm = pl.BlockSpec(memory_space=pl.ANY)

time: 40.8 us -> 37.1 us (0.909)
  Pallas kernels: 38.1 us -> 34.8 us
    pallas_call x1, Pallas kernels: 38.1 us -> 34.8 us  [per_device(): pl.pallas_call(kernel, out_shape=(jax.ShapeDtypeStruct((16, 32, 256), F32...]
where the time goes in v3:
time: 37.1 us; the launch traced here: 36.8 us
  Pallas kernels  34.8 us (94%)
  local copies, waits for them, and re-layouts  1.41 us (4%)
  between operations  0.64 us (2%)
    pallas_call x1, Pallas kernels, per_device(): pl.pallas_call(kernel, out_shape=(jax.ShapeDtypeStruct((16, 32, 256), F32...  34.8 us
    unnamed x2, local copies, waits for them, and re-layouts  1.41 us

profile of v3, /device:TPU:1, one launch (start us, length us, event | category | flops | bytes accessed | tf_op | source)
XLA Modules:
  0.0 36.8 jit_solution(9412337826249191077)
XLA Ops:
  0.6 34.8 %shard_map.41 = (f32[16,32,256]{2,1,0:T(8,128)S(1)}, f32[2,32,64]{2,1,0:T(8,128)S(1)}) custom-call(f32[16,32,256]{2,1,0:T(8,128)} %refs_0_.1, s32[16,32,256]{2,1,0:T(8,128)} %refs_1_.1), custom_call_target="tpu_custom_call" | custom-call | tf_op jit(solution)/shard_map/pallas_call | solution.py:607
  35.4 0.8 %copy.6 = f32[16,32,256]{2,1,0:T(8,128)} copy(f32[16,32,256]{2,1,0:T(8,128)S(1)} %get-tuple-element.8) | data formatting | bytes 1048576
  36.2 0.6 %copy.7 = f32[2,64,32]{1,2,0:T(8,128)} copy(f32[2,64,32]{1,2,0:T(8,128)S(1)} %bitcast.1) | data formatting | bytes 32768

commit v4 on v3

--- a/solution.py
+++ b/solution.py
@@ -16,11 +16,11 @@
 BLOCK = ((16, 32, 256), (8, 16, 128), (4, 8, 64), (2, 64, 32))
 LOW = (4, 4, 12, 5)
 PLANES = (22, 14, 28, 11)
-ROWS = (40, 24, 16, 72)
+ROWS = (40, 32, 16, 16)
 LANES = (256, 128, 128, 128)
 
 NEAR = [(a, b) for a in (-1, 0, 1) for b in (-1, 0, 1) if (a, b) != (0, 0)]
-WIDE = [(a, b) for c in (3, 2, 1, 0) for a in (-c, c)[:1 + (c > 0)] for b in (-1, 1, 0) if (a, b) != (0, 0)]
+WIDE = [(a, 0) for a in (-3, 3, -2, 2, -1, 1)]
 ALONG = [(0, k) for k in (10, 9, 11, 6, 5, 7, 14, 13, 2, 8, 3, 15, 12, 4, 1)]
 
 
@@ -48,6 +48,7 @@
         self.n = BLOCK[index]
         self.low = LOW[index]
         self.rows, self.lanes = ROWS[index], LANES[index]
+        self.edges = index != 2
         self.g, self.l = g, l
 
     def up(self, x, axis):
@@ -58,25 +59,45 @@
 
     def lane_up(self, x):
         y = self.up(x, x.ndim - 1)
-        return jnp.where(lane_ids(y.shape) == self.n[2] - 1, 0.0, y) if self.n[2] == self.lanes else y
+        return jnp.where(self.at_end(y.shape), 0.0, y) if self.edges else y
 
     def lane_down(self, x):
         y = self.down(x, x.ndim - 1)
-        return jnp.where(lane_ids(y.shape) == 0, 0.0, y) if self.n[2] == self.lanes else y
+        return jnp.where(self.at_start(y.shape), 0.0, y) if self.edges else y
+
+    def own_lane(self, shape):
+        lane = lane_ids(shape)
+        return lane & (self.n[2] - 1) if self.index == 3 else lane
+
+    def at_start(self, shape):
+        return self.own_lane(shape) == 0
+
+    def at_end(self, shape):
+        return self.own_lane(shape) == self.n[2] - 1
 
     def row_up(self, x):
-        return self.up(x, x.ndim - 2)
+        y = self.up(x, x.ndim - 2)
+        if self.index < 3:
+            return y
+        tile = y[:, 8:16]
+        after = jnp.where(lane_ids(tile.shape) < 96, pltpu.roll(tile, 96, 2), 0.0)
+        return jnp.concatenate([y[:, 0:8], jnp.where(row_ids(tile.shape) == 7, after, tile)], 1)
 
     def row_down(self, x):
-        return self.down(x, x.ndim - 2)
+        y = self.down(x, x.ndim - 2)
+        if self.index < 3:
+            return y
+        tile = y[:, 0:8]
+        before = jnp.where(lane_ids(tile.shape) >= 32, pltpu.roll(tile, 32, 2), 0.0)
+        return jnp.concatenate([jnp.where(row_ids(tile.shape) == 0, before, tile), y[:, 8:16]], 1)
 
     def row_valid(self, shape):
         r = row_ids(shape)
         if self.index == 3:
-            ok = r < self.n[1]
-        else:
-            j = jnp.where(r < self.n[1] + 4, r, r - self.rows) + self.l * self.n[1]
-            ok = (j >= 0) & (j < WHOLE[self.index][1])
+            return jnp.ones(shape, F32)
+        ahead = self.n[1] + (4, 6, 4)[self.index]
+        j = jnp.where(r < ahead, r, r - self.rows) + self.l * self.n[1]
+        ok = (j >= 0) & (j < WHOLE[self.index][1])
         if self.n[2] < self.lanes:
             ok = ok & (lane_ids(shape) < self.n[2])
         return jnp.where(ok, 1.0, 0.0).astype(F32)
@@ -101,8 +122,8 @@
         pl_, pj, pjl = before
         k = cjl + pjl
         el = cj + pj
-        if self.n[2] == self.lanes:
-            el = jnp.where(lane_ids(el.shape) == self.n[2] - 1, 0.0, el)
+        if self.edges:
+            el = jnp.where(self.at_end(el.shape), 0.0, el)
         return cjl, cl + pl_, el, 5.0 * k, valid * (0.15 / jnp.maximum(k, 1.0))
 
     def parts(self, u):
@@ -230,6 +251,10 @@
     def send(src, dst, s_sem, r_sem, to, wrap=False):
         return Sent(src, dst, s_sem, r_sem, to, wrap)
 
+    def flush(copies):
+        for copy in copies:
+            copy.wait_send()
+
     load_f = pltpu.make_async_copy(rhs, L0.F.at[4:20, 0:32], lsem.at[0])
     load_p = pltpu.make_async_copy(phase, ph, lsem.at[1])
     load_p.start()
@@ -264,8 +289,8 @@
         g == NG - 1, L0.F.at[20:22, 0:32], L0.C.at[20:22, 0:32], L1.F.at[12:14, 0:16], L1.C.at[12:14, 0:16],
         *[x.at[20:22] for x in (rxl0, rxh0)], *[x.at[12:14] for x in near_tiles],
     )
-    clear(l == 0, rxl0, rxl1, crl1, rf2.at[:, 0], rn2.at[:, 0])
-    clear(l == NL - 1, rxh0, rxh1, crh1, rf2.at[:, 2], rn2.at[:, 2])
+    clear(l == 0, rxl0, rxl1, crl1)
+    clear(l == NL - 1, rxh0, rxh1, crh1)
     for d in (1, 2, 3):
         clear(g < d, rf2.at[3 - d], rn2.at[3 - d])
         clear(g >= NG - d, rf2.at[3 + d], rn2.at[3 + d])
@@ -302,7 +327,7 @@
         copies = []
         for k, (dg, dl) in enumerate(NEAR):
             lo, hi, at = {1: (12 - depth, 12, 4 - depth), 0: (4, 12, 4), -1: (4, 6, 12)}[dg]
-            rows, target = {1: (slice(8, 16), low), 0: (slice(0, 16), ref), -1: (slice(0, 8), high)}[dl]
+            rows, target = {1: (slice(0, 16), low), 0: (slice(0, 16), ref), -1: (slice(0, 8), high)}[dl]
             where = pl.ds(at, hi - lo)
             dst = target.at[where, 0:16] if dl == 0 else target.at[where]
             copies.append(send(ref.at[lo:hi, rows], dst, ssem.at[k], rsem.at[k], (dg, dl)))
@@ -310,13 +335,18 @@
 
     def wide_sends(src, slots, ssem, rsem):
         return [
-            send(src, slots.at[3 - dg, 1 - dl], ssem.at[k], rsem.at[k], (dg, dl))
+            send(src, slots.at[3 - dg], ssem.at[k], rsem.at[k], (dg, dl))
             for k, (dg, dl) in enumerate(WIDE)
         ]
 
     def along_sends(src, slots, ssem, rsem):
-        mine = slots.at[lax.div(l, 2), lax.rem(l, 2)]
-        return [send(src, mine, ssem.at[k], rsem.at[k], to, True) for k, to in enumerate(ALONG)]
+        for to in ALONG:
+            pltpu.make_async_remote_copy(
+                src_ref=src, dst_ref=slots.at[l], send_sem=ssem.at[0], recv_sem=rsem.at[0],
+                device_id=device(*to), device_id_type=MESH,
+            ).start()
+        whole = slots.at[0:NL - 1]
+        return [pltpu.make_async_copy(whole, whole, sem.at[0]) for sem in (rsem, ssem)]
 
     greet(known.at[0], NEAR)
 
@@ -338,18 +368,7 @@
     ).reshape(8, 32, 128)
     n1[...] = ct1[:, pl.ds(0, 16, stride=2), :] + ct1[:, pl.ds(1, 16, stride=2), :]
     count1 = n1[...]
-    L1.C[4:12, 0:16] = 1.0 + 124.875 * count1
-    pairs = jnp.concatenate([count1[2 * i:2 * i + 1] + count1[2 * i + 1:2 * i + 2] for i in range(4)], 0)
-    ct2[...] = jnp.dot(
-        pairs.reshape(4 * 16, 128).astype(BF16), p1_mat[...], preferred_element_type=F32
-    ).reshape(4, 16, 128)
-    count2 = ct2[:, pl.ds(0, 8, stride=2), :] + ct2[:, pl.ds(1, 8, stride=2), :]
-    pn2[...] = count2[0:2] + pltpu.roll(count2[2:4], 64, 2)
-    rn2[3, 1] = pn2[...]
-
-    for ref in (L3.F, L3.C):
-        ref[:, 64:72] = jnp.zeros((PLANES[3], 8, 128), F32)
-
+    L1.C[4:12, 0:16] = count1
     got_c1 = near_sends(L1.C, crl1, crh1, sc1, qc1, 4)
     pl.semaphore_wait(known.at[0], around)
     known_1 = greet(known.at[1], [(-1, 0), (1, 0)])
@@ -428,60 +447,69 @@
             coarser_rows(s0.at[half], 16).reshape(8 * 16, 128), r0_mat[128 * half:128 * half + 128]
         )
     L1.F[4:12, 0:16] = total.reshape(8, 16, 128)
+    earlier, sent[:] = sent[:], []
     got_f1 = near_sends(L1.F, rxl1, rxh1, sf1, qf1, 3)
 
     pl.semaphore_wait(known.at[1], known_1)
     pl.semaphore_wait(known.at[2], known_2)
     known_3 = greet(known.at[3], [(0, -4), (0, 4)])
-    got_c2 = wide_sends(pn2, rn2, sc2, qc2)
 
     for copy in got_c1:
         copy.wait_recv()
-    sub1 = row_ids((1, 8, 128)) < 4
-    valid1 = L1.row_valid((1, 24, 128)) * L1.plane_valid_many(0, 14)
-    c1w[:, 0:16] = L1.C[:, 0:16] * valid1[:, 0:16]
-    c1w[:, 16:24] = jnp.where(sub1, crh1[...], crl1[...]) * valid1[:, 16:24]
+    def merge_rows(ref, low, high, lo, hi):
+        inner = row_ids((1, 8, 128)) < 6
+        ref[lo:hi, 16:24] = jnp.where(inner, high[lo:hi], low[lo:hi, 0:8])
+        ref[lo:hi, 24:32] = low[lo:hi, 8:16]
+
+    merge_rows(L1.C, crl1, crh1, 0, 14)
+    for i in range(4):
+        s1[i, 0:32] = L1.C[2 * i + 4] + L1.C[2 * i + 5]
+    pairs = s1[:, pl.ds(0, 16, stride=2), :] + s1[:, pl.ds(1, 16, stride=2), :]
+    count2 = jnp.dot(
+        pairs.reshape(4 * 16, 128).astype(BF16), p1_mat[...], preferred_element_type=F32
+    ).reshape(4, 16, 128)
+    pn2[...] = count2[0:2] + pltpu.roll(count2[2:4], 64, 2)
+    rn2[3] = pn2[...]
+    got_c2 = wide_sends(pn2, rn2, sc2, qc2)
+    valid1 = L1.row_valid((1, 32, 128)) * L1.plane_valid_many(0, 14)
+    c1w[...] = (1.0 + 124.875 * L1.C[...]) * valid1
     L1.C = c1w
     L1.setup_all(1, 14)
 
+    flush(earlier)
     pl.semaphore_wait(known.at[3], known_3)
     known_4 = greet(known.at[4], [(0, -8), (0, 8)])
 
     for copy in got_f1:
         copy.wait_recv()
-    L1.F[1:14, 16:24] = jnp.where(sub1, rxh1[1:14], rxl1[1:14])
+    merge_rows(L1.F, rxl1, rxh1, 1, 14)
     L1.first_all(1, 14)
     L1.sweep_all(L1.U, L1.V, 2, 13)
     r1 = L1.residual_all(L1.V, 3, 12) * valid1[3:12]
-    r1 = jnp.concatenate([r1[:, 16:24], r1[:, 0:16]], 1)
     for i, plane in enumerate(coarser_planes(r1)):
-        s1[i] = plane
-    f2 = split_dot(coarser_rows(s1, 8).reshape(4 * 8, 128), r1_mat[...]).reshape(4, 8, 128)
+        s1[i, 0:8] = plane[24:32]
+        s1[i, 8:40] = plane
+    f2 = split_dot(coarser_rows(s1, 16).reshape(4 * 16, 128), r1_mat[...]).reshape(4, 16, 128)
     pf2[...] = f2[0:2] + pltpu.roll(f2[2:4], 64, 2)
-    rf2[3, 1] = pf2[...]
+    rf2[3] = pf2[...]
+    earlier, sent[:] = sent[:], []
     got_f2 = wide_sends(pf2, rf2, sf2, qf2)
 
     pl.semaphore_wait(known.at[4], known_4)
 
-    def unpack_wide(slots, put):
+    def unpack_wide(slots, ref):
         lane = lane_ids((1, 1, 1, 128)) < 64
-        own = slots[:, 1]
-        halo = jnp.where(row_ids((1, 1, 8, 128)) < 4, slots[:, 2], slots[:, 0])
-        for tile, rows in ((own, slice(0, 8)), (halo, slice(8, 16))):
-            first = jnp.where(lane, tile, 0.0)
-            later = jnp.where(lane, pltpu.roll(tile, 64, 3), 0.0)
-            for d in range(7):
-                for half in range(2):
-                    put(4 * d + half, rows, first[d, half])
-                    put(4 * d + 2 + half, rows, later[d, half])
+        tiles = slots[...]
+        first = jnp.where(lane, tiles, 0.0)
+        later = jnp.where(lane, pltpu.roll(tiles, 64, 3), 0.0)
+        for d in range(7):
+            ref[4 * d:4 * d + 2] = first[d]
+            ref[4 * d + 2:4 * d + 4] = later[d]
 
     for copy in got_c2:
         copy.wait_recv()
 
-    def put_n2(i, rows, value):
-        n2w[i, rows] = value
-
-    unpack_wide(rn2, put_n2)
+    unpack_wide(rn2, n2w)
     valid2 = L2.row_valid((1, 16, 128)) * L2.plane_valid_many(0, 28)
     L2.C[...] = (1.0 + (999.0 / 64.0) * n2w[...]) * valid2
     L2.setup_all(1, 26)
@@ -492,8 +520,6 @@
         pairs.reshape(11 * 8, 128).astype(BF16), p1_mat[...], preferred_element_type=F32
     ).reshape(11, 8, 128)
     count3 = n3s[:, pl.ds(0, 4, stride=2), :] + n3s[:, pl.ds(1, 4, stride=2), :]
-
-    odd = lax.rem(l, 2) == 1
 
     def pack(planes, ref):
         for t in range(2):
@@ -505,30 +531,35 @@
                         total = total + (pltpu.roll(planes[p], 32 * q, 1) if q else planes[p])
                 ref[t, 4 * h:4 * h + 4] = total
         tiles = ref[...]
-        ref[...] = jnp.where(odd, pltpu.roll(tiles, 4, 1), tiles)
+        tiles = jnp.where(lax.rem(l, 2) == 1, pltpu.roll(tiles, 4, 1), tiles)
+        tiles = jnp.where(lax.rem(lax.div(l, 4), 2) == 1, pltpu.roll(tiles, 32, 2), tiles)
+        ref[...] = jnp.where(l >= 8, pltpu.roll(tiles, 64, 2), tiles)
 
     def unpack_along(slots, count, put):
-        sub = row_ids((1, 8, 128)) < 4
-        lane = lane_ids((1, 8, 128)) < 32
+        half, group = row_ids((8, 128)) // 4, lane_ids((8, 128)) // 32
+        cell = [[(half == h) & (group == q) for q in range(4)] for h in range(2)]
         for p in range(count):
             t, h, q = p // 8, (p % 8) // 4, p % 4
-            even, other = slots[:, 0, t], slots[:, 1, t]
-            tile = jnp.where(sub, even, other) if h == 0 else pltpu.roll(jnp.where(sub, other, even), 4, 1)
-            if q:
-                tile = pltpu.roll(tile, 128 - 32 * q, 2)
-            put(p, jnp.where(lane, tile, 0.0).reshape(64, 128))
+            for tile in range(2):
+                total = slots[2 * tile, t]
+                for owner in range(1, 8):
+                    e, o = owner % 2, owner // 2
+                    total = jnp.where(cell[(h + e) % 2][(q + o) % 4], slots[4 * o + 2 * tile + e, t], total)
+                if h:
+                    total = pltpu.roll(total, 4, 0)
+                if q:
+                    total = pltpu.roll(total, 128 - 32 * q, 1)
+                put(p, slice(8 * tile, 8 * tile + 8), total)
 
     pack([count3[i] for i in range(11)], pc3)
-    rc3[lax.div(l, 2), lax.rem(l, 2)] = pc3[...]
+    rc3[l] = pc3[...]
     got_c3 = along_sends(pc3, rc3, sc3, qc3)
+    flush(earlier)
 
     for copy in got_f2:
         copy.wait_recv()
 
-    def put_f2(i, rows, value):
-        L2.F[i, rows] = value
-
-    unpack_wide(rf2, put_f2)
+    unpack_wide(rf2, L2.F)
     L2.first_all(1, 26)
     L2.sweep_all(L2.U, L2.V, 2, 25)
     r2 = L2.residual_all(L2.V, 3, 24) * valid2[3:24]
@@ -537,25 +568,23 @@
         s2[i, 8:24] = plane
     f3 = split_dot(coarser_rows(s2, 8).reshape(10 * 8, 128), r2_mat[...]).reshape(10, 8, 128)
     pack([f3[i, 0:4] for i in range(10)], pf3)
-    rf3[lax.div(l, 2), lax.rem(l, 2)] = pf3[...]
+    rf3[l] = pf3[...]
+    earlier = sent[:]
     got_f3 = along_sends(pf3, rf3, sf3, qf3)
 
-    for copy in got_c3:
-        copy.wait_recv()
-
-    def put_c3(p, value):
-        L3.C[p, 0:64] = (1.0 + (999.0 / 512.0) * value) * (
-            L3.row_valid((72, 128))[0:64] * L3.plane_valid(p)
-        )
+    flush(earlier)
+    got_c3[0].wait()
+
+    def put_c3(p, rows, value):
+        L3.C[p, rows] = (1.0 + (999.0 / 512.0) * value) * L3.plane_valid(p)
 
     unpack_along(rc3, 11, put_c3)
     L3.setup_all(1, 11)
 
-    for copy in got_f3:
-        copy.wait_recv()
-
-    def put_f3(p, value):
-        L3.F[p + 1, 0:64] = value
+    got_f3[0].wait()
+
+    def put_f3(p, rows, value):
+        L3.F[p + 1, rows] = value
 
     unpack_along(rf3, 10, put_f3)
     L3.first_all(1, 11)
@@ -565,11 +594,12 @@
         source, target = target, source
     last = (8.0 / 12.0) * L3.residual_all(source, 5, 7)
     for i in range(2):
-        coarse_out[i] = jnp.transpose(last[i, 0:64], (1, 0))[0:32]
+        turned = jnp.transpose(last[i], (1, 0))
+        coarse_out[i] = jnp.concatenate([turned[32 * q:32 * q + 32] for q in range(4)], 1)
 
     store.wait()
-    for copy in sent:
-        copy.wait_send()
+    got_c3[1].wait()
+    got_f3[1].wait()
 
 
 def per_device(right_side, phase):
@@ -586,21 +616,21 @@
             ((17, 2, 40, 128), F32), ((2, 8, 40, 128), F32),
             ((16, 32, 256), F32),
             ((8, 32, 128), F32), ((8, 16, 128), F32), ((17, 16, 128), F32),
-            ((14, 8, 128), F32), ((14, 8, 128), F32), ((14, 8, 128), F32), ((14, 8, 128), F32),
-            ((14, 24, 128), F32),
-            ((4, 24, 128), F32),
+            ((14, 16, 128), F32), ((14, 8, 128), F32), ((14, 16, 128), F32), ((14, 8, 128), F32),
+            ((14, 32, 128), F32),
+            ((4, 40, 128), F32),
             ((4, 16, 128), F32),
-            ((2, 8, 128), F32), ((2, 8, 128), F32),
-            ((7, 3, 2, 8, 128), F32), ((7, 3, 2, 8, 128), F32),
+            ((2, 16, 128), F32), ((2, 16, 128), F32),
+            ((7, 2, 16, 128), F32), ((7, 2, 16, 128), F32),
             ((28, 16, 128), F32), ((11, 8, 128), F32), ((10, 24, 128), F32),
             ((2, 8, 128), F32), ((2, 8, 128), F32),
-            ((8, 2, 2, 8, 128), F32), ((8, 2, 2, 8, 128), F32),
+            ((16, 2, 8, 128), F32), ((16, 2, 8, 128), F32),
             ((256, 128), BF16), ((128, 128), BF16), ((128, 128), BF16),
             ((256, 128), BF16), ((128, 128), BF16),
         )
     ]
     scratch += [pltpu.SemaphoreType.DMA((3,)), pltpu.SemaphoreType.REGULAR((5,))]
-    for n in (12, len(NEAR), len(NEAR), len(WIDE), len(WIDE), len(ALONG), len(ALONG)):
+    for n in (12, len(NEAR), len(NEAR), len(WIDE), len(WIDE), 1, 1):
         scratch += [pltpu.SemaphoreType.DMA((n,)), pltpu.SemaphoreType.DMA((n,))]
     vmem = pl.BlockSpec(memory_space=pltpu.VMEM)
     hbm = pl.BlockSpec(memory_space=pl.ANY)

time: 37.1 us -> 34.6 us (0.933)
  Pallas kernels: 34.8 us -> 32.4 us
    pallas_call x1, Pallas kernels: 34.8 us -> 32.4 us  [per_device(): pl.pallas_call(kernel, out_shape=(jax.ShapeDtypeStruct((16, 32, 256), F32...]
where the time goes in v4:
time: 34.6 us; the launch traced here: 34.4 us
  Pallas kernels  32.4 us (94%)
  local copies, waits for them, and re-layouts  1.41 us (4%)
  between operations  0.64 us (2%)
    pallas_call x1, Pallas kernels, per_device(): pl.pallas_call(kernel, out_shape=(jax.ShapeDtypeStruct((16, 32, 256), F32...  32.4 us
    unnamed x2, local copies, waits for them, and re-layouts  1.41 us

profile of v4, /device:TPU:1, one launch (start us, length us, event | category | flops | bytes accessed | tf_op | source)
XLA Modules:
  0.0 34.4 jit_solution(2769324097828955684)
XLA Ops:
  0.6 32.4 %shard_map.41 = (f32[16,32,256]{2,1,0:T(8,128)S(1)}, f32[2,32,64]{2,1,0:T(8,128)S(1)}) custom-call(f32[16,32,256]{2,1,0:T(8,128)} %refs_0_.1, s32[16,32,256]{2,1,0:T(8,128)} %refs_1_.1), custom_call_target="tpu_custom_call" | custom-call | tf_op jit(solution)/shard_map/pallas_call | solution.py:637
  33.0 0.8 %copy.6 = f32[16,32,256]{2,1,0:T(8,128)} copy(f32[16,32,256]{2,1,0:T(8,128)S(1)} %get-tuple-element.8) | data formatting | bytes 1048576
  33.8 0.6 %copy.7 = f32[2,64,32]{1,2,0:T(8,128)} copy(f32[2,64,32]{1,2,0:T(8,128)S(1)} %bitcast.1) | data formatting | bytes 32768

commit v5 on v4

--- a/solution.py
+++ b/solution.py
@@ -20,6 +20,7 @@
 LANES = (256, 128, 128, 128)
 
 NEAR = [(a, b) for a in (-1, 0, 1) for b in (-1, 0, 1) if (a, b) != (0, 0)]
+FACES = [(0, 1), (0, -1), (1, 0), (-1, 0)]
 WIDE = [(a, 0) for a in (-3, 3, -2, 2, -1, 1)]
 ALONG = [(0, k) for k in (10, 9, 11, 6, 5, 7, 14, 13, 2, 8, 3, 15, 12, 4, 1)]
 
@@ -272,7 +273,7 @@
             count = count + jnp.where(test, 1, 0)
         return count
 
-    around = greet(barrier, NEAR)
+    around = greet(barrier, FACES)
 
     def clear(test, *refs):
         @pl.when(test)
@@ -305,23 +306,21 @@
     pl.semaphore_wait(barrier, around)
 
     first = []
-    k = 0
     for src, dst, to in (
-        (upk.at[0:8], rxl0.at[4:12], (0, 1)),
-        (dpk.at[0:8], rxh0.at[4:12], (0, -1)),
-        (upk.at[8:16], rxl0.at[12:20], (0, 1)),
-        (dpk.at[8:16], rxh0.at[12:20], (0, -1)),
+        (upk.at[0:4], rxl0.at[4:8], (0, 1)),
+        (dpk.at[0:4], rxh0.at[4:8], (0, -1)),
+        (upk.at[4:8], rxl0.at[8:12], (0, 1)),
+        (dpk.at[4:8], rxh0.at[8:12], (0, -1)),
+        (upk.at[8:12], rxl0.at[12:16], (0, 1)),
+        (dpk.at[8:12], rxh0.at[12:16], (0, -1)),
+        (upk.at[12:16], rxl0.at[16:20], (0, 1)),
+        (dpk.at[12:16], rxh0.at[16:20], (0, -1)),
         (L0.C.at[16:20, 0:32], L0.C.at[0:4, 0:32], (1, 0)),
         (L0.F.at[17:20, 0:32], L0.F.at[1:4, 0:32], (1, 0)),
         (L0.C.at[4:6, 0:32], L0.C.at[20:22, 0:32], (-1, 0)),
         (L0.F.at[4:6, 0:32], L0.F.at[20:22, 0:32], (-1, 0)),
-        (upk.at[12:16], rxl0.at[0:4], (1, 1)),
-        (dpk.at[12:16], rxh0.at[0:4], (1, -1)),
-        (upk.at[0:2], rxl0.at[20:22], (-1, 1)),
-        (dpk.at[0:2], rxh0.at[20:22], (-1, -1)),
     ):
-        first.append(send(src, dst, ss0.at[k], rs0.at[k], to))
-        k += 1
+        first.append(send(src, dst, ss0.at[len(first)], rs0.at[len(first)], to))
 
     def near_sends(ref, low, high, ssem, rsem, depth):
         copies = []
@@ -348,7 +347,7 @@
         whole = slots.at[0:NL - 1]
         return [pltpu.make_async_copy(whole, whole, sem.at[0]) for sem in (rsem, ssem)]
 
-    greet(known.at[0], NEAR)
+    greet(known.at[0], FACES)
 
     weights = ((r0_mat, 256), (r1_mat, 128), (r2_mat, 64))
     for ref, used in weights:
@@ -369,8 +368,15 @@
     n1[...] = ct1[:, pl.ds(0, 16, stride=2), :] + ct1[:, pl.ds(1, 16, stride=2), :]
     count1 = n1[...]
     L1.C[4:12, 0:16] = count1
+    pl.semaphore_wait(known.at[0], around)
+    for src, dst, to in (
+        (upk.at[12:16], rxl0.at[0:4], (1, 1)),
+        (dpk.at[12:16], rxh0.at[0:4], (1, -1)),
+        (upk.at[0:2], rxl0.at[20:22], (-1, 1)),
+        (dpk.at[0:2], rxh0.at[20:22], (-1, -1)),
+    ):
+        first.append(send(src, dst, ss0.at[len(first)], rs0.at[len(first)], to))
     got_c1 = near_sends(L1.C, crl1, crh1, sc1, qc1, 4)
-    pl.semaphore_wait(known.at[0], around)
     known_1 = greet(known.at[1], [(-1, 0), (1, 0)])
     known_2 = greet(known.at[2], [(0, -2), (0, 2)])
 
@@ -406,18 +412,28 @@
         L0.Ei[lo - 1] = before[2]
         L0.planes_loop(lo, hi, setup, before, 8)
 
-    for copy in first[:2]:
-        copy.wait_recv()
-    lax.fori_loop(4, 12, merge, 0)
-    setup_planes(5, 12)
-    L0.apply_loop(L0.U, 6, 11, second, 6)
+    for copy in first[0:2]:
+        copy.wait_recv()
+    lax.fori_loop(4, 8, merge, 0)
+    setup_planes(5, 8)
+    L0.apply_loop(L0.U, 6, 7, second, 8)
     for copy in first[2:4]:
         copy.wait_recv()
-    lax.fori_loop(12, 20, merge, 0)
-    setup_planes(12, 20)
-    L0.apply_loop(L0.U, 11, 19, second, 4)
+    lax.fori_loop(8, 12, merge, 0)
+    setup_planes(8, 12)
+    L0.apply_loop(L0.U, 7, 11, second, 8)
+    for copy in first[4:6]:
+        copy.wait_recv()
+    lax.fori_loop(12, 16, merge, 0)
+    setup_planes(12, 16)
+    L0.apply_loop(L0.U, 11, 15, second, 8)
+    for copy in first[6:8]:
+        copy.wait_recv()
+    lax.fori_loop(16, 20, merge, 0)
+    setup_planes(16, 20)
+    L0.apply_loop(L0.U, 15, 19, second, 8)
     L0.apply_loop(L0.V, 7, 18, residual, 6)
-    for copy in first[4:]:
+    for copy in first[8:]:
         copy.wait_recv()
     for i in (0, 1, 2, 3, 20, 21):
         merge(i, 0)
@@ -630,7 +646,7 @@
         )
     ]
     scratch += [pltpu.SemaphoreType.DMA((3,)), pltpu.SemaphoreType.REGULAR((5,))]
-    for n in (12, len(NEAR), len(NEAR), len(WIDE), len(WIDE), 1, 1):
+    for n in (16, len(NEAR), len(NEAR), len(WIDE), len(WIDE), 1, 1):
         scratch += [pltpu.SemaphoreType.DMA((n,)), pltpu.SemaphoreType.DMA((n,))]
     vmem = pl.BlockSpec(memory_space=pltpu.VMEM)
     hbm = pl.BlockSpec(memory_space=pl.ANY)

time: 34.6 us -> 34.1 us (0.986)
  the two profiles are of different devices: /device:TPU:1 before, /device:TPU:65 now
where the time goes in v5:
time: 34.1 us; the launch traced here: 34 us
  Pallas kernels  32 us (94%)
  local copies, waits for them, and re-layouts  1.41 us (4%)
  between operations  0.64 us (2%)
    pallas_call x1, Pallas kernels, per_device(): pl.pallas_call(kernel, out_shape=(jax.ShapeDtypeStruct((16, 32, 256), F32...  32 us
    unnamed x2, local copies, waits for them, and re-layouts  1.41 us

profile of v5, /device:TPU:65, one launch (start us, length us, event | category | flops | bytes accessed | tf_op | source)
XLA Modules:
  0.0 34.0 jit_solution(29671814788397587)
XLA Ops:
  0.6 32.0 %shard_map.41 = (f32[16,32,256]{2,1,0:T(8,128)S(1)}, f32[2,32,64]{2,1,0:T(8,128)S(1)}) custom-call(f32[16,32,256]{2,1,0:T(8,128)} %refs_0_.1, s32[16,32,256]{2,1,0:T(8,128)} %refs_1_.1), custom_call_target="tpu_custom_call" | custom-call | tf_op jit(solution)/shard_map/pallas_call | solution.py:653
  32.6 0.8 %copy.6 = f32[16,32,256]{2,1,0:T(8,128)} copy(f32[16,32,256]{2,1,0:T(8,128)S(1)} %get-tuple-element.8) | data formatting | bytes 1048576
  33.4 0.6 %copy.7 = f32[2,64,32]{1,2,0:T(8,128)} copy(f32[2,64,32]{1,2,0:T(8,128)S(1)} %bitcast.1) | data formatting | bytes 32768

commit v6 on v5

--- a/solution.py
+++ b/solution.py
@@ -19,7 +19,7 @@
 ROWS = (40, 32, 16, 16)
 LANES = (256, 128, 128, 128)
 
-NEAR = [(a, b) for a in (-1, 0, 1) for b in (-1, 0, 1) if (a, b) != (0, 0)]
+NEAR = [(1, 1), (1, -1), (-1, 1), (-1, -1), (0, 1), (0, -1), (1, 0), (-1, 0)]
 FACES = [(0, 1), (0, -1), (1, 0), (-1, 0)]
 WIDE = [(a, 0) for a in (-3, 3, -2, 2, -1, 1)]
 ALONG = [(0, k) for k in (10, 9, 11, 6, 5, 7, 14, 13, 2, 8, 3, 15, 12, 4, 1)]
@@ -309,16 +309,16 @@
     for src, dst, to in (
         (upk.at[0:4], rxl0.at[4:8], (0, 1)),
         (dpk.at[0:4], rxh0.at[4:8], (0, -1)),
+        (L0.C.at[16:20, 0:32], L0.C.at[0:4, 0:32], (1, 0)),
+        (L0.F.at[17:20, 0:32], L0.F.at[1:4, 0:32], (1, 0)),
+        (L0.C.at[4:6, 0:32], L0.C.at[20:22, 0:32], (-1, 0)),
+        (L0.F.at[4:6, 0:32], L0.F.at[20:22, 0:32], (-1, 0)),
         (upk.at[4:8], rxl0.at[8:12], (0, 1)),
         (dpk.at[4:8], rxh0.at[8:12], (0, -1)),
         (upk.at[8:12], rxl0.at[12:16], (0, 1)),
         (dpk.at[8:12], rxh0.at[12:16], (0, -1)),
         (upk.at[12:16], rxl0.at[16:20], (0, 1)),
         (dpk.at[12:16], rxh0.at[16:20], (0, -1)),
-        (L0.C.at[16:20, 0:32], L0.C.at[0:4, 0:32], (1, 0)),
-        (L0.F.at[17:20, 0:32], L0.F.at[1:4, 0:32], (1, 0)),
-        (L0.C.at[4:6, 0:32], L0.C.at[20:22, 0:32], (-1, 0)),
-        (L0.F.at[4:6, 0:32], L0.F.at[20:22, 0:32], (-1, 0)),
     ):
         first.append(send(src, dst, ss0.at[len(first)], rs0.at[len(first)], to))
 
@@ -376,7 +376,6 @@
         (dpk.at[0:2], rxh0.at[20:22], (-1, -1)),
     ):
         first.append(send(src, dst, ss0.at[len(first)], rs0.at[len(first)], to))
-    got_c1 = near_sends(L1.C, crl1, crh1, sc1, qc1, 4)
     known_1 = greet(known.at[1], [(-1, 0), (1, 0)])
     known_2 = greet(known.at[2], [(0, -2), (0, 2)])
 
@@ -417,23 +416,24 @@
     lax.fori_loop(4, 8, merge, 0)
     setup_planes(5, 8)
     L0.apply_loop(L0.U, 6, 7, second, 8)
-    for copy in first[2:4]:
+    for copy in first[6:8]:
         copy.wait_recv()
     lax.fori_loop(8, 12, merge, 0)
     setup_planes(8, 12)
     L0.apply_loop(L0.U, 7, 11, second, 8)
-    for copy in first[4:6]:
+    for copy in first[8:10]:
         copy.wait_recv()
     lax.fori_loop(12, 16, merge, 0)
     setup_planes(12, 16)
     L0.apply_loop(L0.U, 11, 15, second, 8)
-    for copy in first[6:8]:
+    for copy in first[10:12]:
         copy.wait_recv()
     lax.fori_loop(16, 20, merge, 0)
     setup_planes(16, 20)
     L0.apply_loop(L0.U, 15, 19, second, 8)
     L0.apply_loop(L0.V, 7, 18, residual, 6)
-    for copy in first[8:]:
+    got_c1 = near_sends(L1.C, crl1, crh1, sc1, qc1, 4)
+    for copy in first[2:6] + first[12:]:
         copy.wait_recv()
     for i in (0, 1, 2, 3, 20, 21):
         merge(i, 0)

time: 34.1 us -> 34.1 us (level)
  the two profiles are of different devices: /device:TPU:65 before, /device:TPU:1 now
where the time goes in v6:
time: 34.1 us; the launch traced here: 33.7 us
  Pallas kernels  31.6 us (93%)
  local copies, waits for them, and re-layouts  1.41 us (4%)
  between operations  0.64 us (2%)
    pallas_call x1, Pallas kernels, per_device(): pl.pallas_call(kernel, out_shape=(jax.ShapeDtypeStruct((16, 32, 256), F32...  31.6 us
    unnamed x2, local copies, waits for them, and re-layouts  1.41 us

profile of v6, /device:TPU:1, one launch (start us, length us, event | category | flops | bytes accessed | tf_op | source)
XLA Modules:
  0.0 33.7 jit_solution(8274902783123466707)
XLA Ops:
  0.6 31.6 %shard_map.41 = (f32[16,32,256]{2,1,0:T(8,128)S(1)}, f32[2,32,64]{2,1,0:T(8,128)S(1)}) custom-call(f32[16,32,256]{2,1,0:T(8,128)} %refs_0_.1, s32[16,32,256]{2,1,0:T(8,128)} %refs_1_.1), custom_call_target="tpu_custom_call" | custom-call | tf_op jit(solution)/shard_map/pallas_call | solution.py:653
  32.3 0.8 %copy.6 = f32[16,32,256]{2,1,0:T(8,128)} copy(f32[16,32,256]{2,1,0:T(8,128)S(1)} %get-tuple-element.8) | data formatting | bytes 1048576
  33.1 0.6 %copy.7 = f32[2,64,32]{1,2,0:T(8,128)} copy(f32[2,64,32]{1,2,0:T(8,128)S(1)} %bitcast.1) | data formatting | bytes 32768

commit v7 on v6

--- a/solution.py
+++ b/solution.py
@@ -445,7 +445,6 @@
     L0.apply_loop(L0.V, 3, 7, residual, 4)
     L0.apply_loop(L0.V, 18, 20, residual, 4)
     store = pltpu.make_async_copy(out, fine_out, lsem.at[2])
-    store.start()
 
     def coarser_planes(r):
         return [0.5 * (r[2 * i] + r[2 * i + 2]) + r[2 * i + 1] for i in range((r.shape[0] - 1) // 2)]
@@ -465,6 +464,7 @@
     L1.F[4:12, 0:16] = total.reshape(8, 16, 128)
     earlier, sent[:] = sent[:], []
     got_f1 = near_sends(L1.F, rxl1, rxh1, sf1, qf1, 3)
+    store.start()
 
     pl.semaphore_wait(known.at[1], known_1)
     pl.semaphore_wait(known.at[2], known_2)
@@ -507,9 +507,9 @@
         s1[i, 8:40] = plane
     f2 = split_dot(coarser_rows(s1, 16).reshape(4 * 16, 128), r1_mat[...]).reshape(4, 16, 128)
     pf2[...] = f2[0:2] + pltpu.roll(f2[2:4], 64, 2)
-    rf2[3] = pf2[...]
     earlier, sent[:] = sent[:], []
     got_f2 = wide_sends(pf2, rf2, sf2, qf2)
+    rf2[3] = pf2[...]
 
     pl.semaphore_wait(known.at[4], known_4)
 
@@ -584,9 +584,9 @@
         s2[i, 8:24] = plane
     f3 = split_dot(coarser_rows(s2, 8).reshape(10 * 8, 128), r2_mat[...]).reshape(10, 8, 128)
     pack([f3[i, 0:4] for i in range(10)], pf3)
-    rf3[l] = pf3[...]
     earlier = sent[:]
     got_f3 = along_sends(pf3, rf3, sf3, qf3)
+    rf3[l] = pf3[...]
 
     flush(earlier)
     got_c3[0].wait()

time: 34.1 us -> 33.8 us (level); the launches traced: 33.7 us -> 33.7 us
  no operation moved by 1% of the time
where the time goes in v7:
time: 33.8 us; the launch traced here: 33.7 us
  Pallas kernels  31.7 us (94%)
  local copies, waits for them, and re-layouts  1.41 us (4%)
  between operations  0.64 us (2%)
    pallas_call x1, Pallas kernels, per_device(): pl.pallas_call(kernel, out_shape=(jax.ShapeDtypeStruct((16, 32, 256), F32...  31.7 us
    unnamed x2, local copies, waits for them, and re-layouts  1.41 us

profile of v7, /device:TPU:1, one launch (start us, length us, event | category | flops | bytes accessed | tf_op | source)
XLA Modules:
  0.0 33.7 jit_solution(15171178043692045598)
XLA Ops:
  0.6 31.7 %shard_map.41 = (f32[16,32,256]{2,1,0:T(8,128)S(1)}, f32[2,32,64]{2,1,0:T(8,128)S(1)}) custom-call(f32[16,32,256]{2,1,0:T(8,128)} %refs_0_.1, s32[16,32,256]{2,1,0:T(8,128)} %refs_1_.1), custom_call_target="tpu_custom_call" | custom-call | tf_op jit(solution)/shard_map/pallas_call | solution.py:653
  32.3 0.8 %copy.6 = f32[16,32,256]{2,1,0:T(8,128)} copy(f32[16,32,256]{2,1,0:T(8,128)S(1)} %get-tuple-element.8) | data formatting | bytes 1048576
  33.1 0.6 %copy.7 = f32[2,64,32]{1,2,0:T(8,128)} copy(f32[2,64,32]{1,2,0:T(8,128)S(1)} %bitcast.1) | data formatting | bytes 32768
